TPU v7x, 32 devices: a whole 2x2x4 slice. The times are simulated.
32 devices in a mesh: exp: 8 (over y, x, core), dp: 4 (over z).
Axes of the slice: x: 2, y: 2, z: 4, core: 2. Of those that a mesh axis runs over, the one named last changes fastest.
Arguments:
- hidden_in: bfloat16 [4096, 768], P(('exp', 'dp')), may hold values from -6 to 6
- cotangent: bfloat16 [4096, 768], P(('exp', 'dp')), may hold values from -6 to 6
- lengths: int32 [32, 3], P(('exp', 'dp')), may hold values from 1 to 96, 128 in all within a row
- routes: int32 [4096, 1], P(('exp', 'dp')), may hold values from 0 to 15; in each aligned block of 128 rows (0 to 127, 128 to 255, ...) at most 10 rows name the same one
- gain_attn: float32 [768], replicated, may hold values from 0.5 to 1.5
- attn_qkv: bfloat16 [768, 2304], P(('exp', 'dp')), may hold values from -0.21875 to 0.21875
- attn_out: bfloat16 [768, 768], P(('exp', 'dp')), may hold values from -0.875 to 0.875
- rel_bias: float32 [32, 12], replicated, may hold values from -3 to 3
- gain_ffn: float32 [768], replicated, may hold values from 0.5 to 1.5
- router: bfloat16 [768, 16], P(('exp', 'dp')), may hold values from -0.109375 to 0.109375
- expert_in: bfloat16 [16, 768, 3072], P('exp', None, 'dp'), may hold values from -0.21875 to 0.21875
- expert_out: bfloat16 [16, 3072, 768], P('exp', 'dp'), may hold values from -2.875 to 2.875
Outputs:
- mixed: bfloat16 [4096, 768], P(('exp', 'dp'))
- grad_in: float32 [4096, 768], P(('exp', 'dp'))
- grad_gain_attn: float32 [768], replicated
- grad_attn_qkv: float32 [768, 2304], P(('exp', 'dp'))
- grad_attn_out: float32 [768, 768], P(('exp', 'dp'))
- grad_rel_bias: float32 [32, 12], replicated
- grad_gain_ffn: float32 [768], replicated
- grad_router: float32 [768, 16], P(('exp', 'dp'))
- grad_expert_in: float32 [16, 768, 3072], P('exp', None, 'dp')
- grad_expert_out: float32 [16, 3072, 768], P('exp', 'dp')
Inputs may be any that keep to these rules, and one draw needn't show every extreme that they name: `routes`: in the rows of one device no expert is named by more than 10 rows. The 3 lengths of one device sum to 128.
All inputs are finite; a program needn't handle non-finite values.
Results may differ from a plain program's by a relative error of at most 0.019.
Values may be sent and summed in bfloat16 or wider, within the bound.
A program may use at most 128 MiB of HBM per device.

v0:
```python
import jax
import jax.numpy as jnp
import numpy as np
from jax import lax
from jax.sharding import PartitionSpec as P

epsilon = 1e-06


def bucket_table(row_count, bucket_count):
    offset = np.arange(row_count)[None, :] - np.arange(row_count)[:, None]
    half_count = bucket_count // 2
    exact_count = half_count // 2
    spread = np.abs(offset)
    scaled = (
        np.log(np.maximum(spread, 1) / exact_count)
        / np.log(128.0 / exact_count)
        * (half_count - exact_count)
    )
    distant = np.minimum(exact_count + np.maximum(scaled, 0.0).astype(np.int32), half_count - 1)
    return ((offset > 0) * half_count + np.where(spread < exact_count, spread, distant)).astype(
        np.int32
    )


def rms_norm(values, gain_vec):
    return (
        values * lax.rsqrt(jnp.mean(values * values, axis=-1, keepdims=True) + epsilon) * gain_vec
    )


def gelu_tanh(values):
    return jax.nn.gelu(values, approximate=True)


def segment_ids(lengths, row_count):
    boundary = jnp.cumsum(lengths, axis=-1)
    position = jnp.arange(row_count, dtype=jnp.int32)
    return jnp.sum((position[:, None] >= boundary[..., None, :]).astype(jnp.int32), axis=-1)


def score_block(queries, key_rows, pos_bias, allowed, score_scale):
    scores = (
        jnp.einsum("qhe,khe->hqk", queries, key_rows, preferred_element_type=jnp.float32)
        * score_scale
        + pos_bias
    )
    return jnp.where(allowed, scores, -1e30)


def local(
    hidden_in,
    cotangent,
    lengths,
    routes,
    gain_attn,
    attn_qkv,
    attn_out,
    rel_bias,
    gain_ffn,
    router,
    expert_in,
    expert_out,
):
    row_count, model_width = hidden_in.shape
    bucket_count, head_count = rel_bias.shape
    head_size = model_width // head_count
    score_scale = head_size ** (-0.5)
    expert_count = router.shape[1]
    group_count = lax.axis_size("exp")
    local_count = expert_in.shape[0]
    capacity = max(2, row_count * 5 // (4 * expert_count))
    full_qkv, full_out, full_route = (
        lax.all_gather(attn_qkv, ("exp", "dp"), axis=0, tiled=True),
        lax.all_gather(attn_out, ("exp", "dp"), axis=0, tiled=True),
        lax.all_gather(router, ("exp", "dp"), axis=0, tiled=True),
    )
    inputs = hidden_in.astype(jnp.float32)
    normed, attn_norm_pull = jax.vjp(rms_norm, inputs, gain_attn)
    normed_low = normed.astype(jnp.bfloat16)
    qkv_low = jnp.dot(normed_low, full_qkv, preferred_element_type=jnp.float32).astype(jnp.bfloat16)
    queries = qkv_low[:, :model_width].reshape(row_count, head_count, head_size)
    key_rows = qkv_low[:, model_width : 2 * model_width].reshape(row_count, head_count, head_size)
    value_rows = qkv_low[:, 2 * model_width :].reshape(row_count, head_count, head_size)
    bucket_ids = bucket_table(row_count, bucket_count)
    pos_bias = jnp.transpose(jnp.take(rel_bias, bucket_ids, axis=0), (2, 0, 1))
    segment = segment_ids(lengths, row_count)[0]
    allowed = (segment[:, None] == segment[None, :])[None]
    scores = score_block(queries, key_rows, pos_bias, allowed, score_scale)
    row_max = jnp.max(scores, axis=-1, keepdims=True)
    log_total = row_max + jnp.log(jnp.sum(jnp.exp(scores - row_max), axis=-1, keepdims=True))
    attn_probs = jnp.exp(scores - log_total)
    attended = jnp.einsum(
        "hqk,khe->qhe",
        attn_probs.astype(jnp.bfloat16),
        value_rows,
        preferred_element_type=jnp.float32,
    )
    attended_low = attended.reshape(row_count, model_width).astype(jnp.bfloat16)
    middle = inputs + jnp.dot(attended_low, full_out, preferred_element_type=jnp.float32)
    ffn_norm, ffn_norm_pull = jax.vjp(rms_norm, middle, gain_ffn)
    ffn_low = ffn_norm.astype(jnp.bfloat16)
    gate_probs = jax.nn.softmax(
        jnp.dot(ffn_low, full_route, preferred_element_type=jnp.float32), axis=-1
    )
    choose = routes == jnp.arange(expert_count, dtype=jnp.int32)[None, :]
    gate_prob = jnp.sum(jnp.where(choose, gate_probs, 0.0), axis=1, keepdims=True)
    rank_index = jnp.cumsum(choose.astype(jnp.int32), axis=0) - 1
    slot_index = jnp.sum(jnp.where(choose, rank_index, 0), axis=1)
    slot_place = routes[:, 0] * capacity + slot_index
    dispatch = (
        jnp.arange(expert_count * capacity, dtype=jnp.int32)[:, None] == slot_place[None, :]
    ).astype(jnp.bfloat16)
    outgoing = jnp.dot(dispatch, ffn_low, preferred_element_type=jnp.float32).astype(jnp.bfloat16)
    outgoing = outgoing.reshape(group_count, local_count, capacity, model_width)
    arrived = lax.all_to_all(outgoing, "exp", split_axis=0, concat_axis=0, tiled=True)
    expert_rows = lax.all_gather(arrived[None], "dp", axis=0, tiled=True)
    hidden_pre = jnp.einsum(
        "rslcd,ldf->rslcf", expert_rows, expert_in, preferred_element_type=jnp.float32
    )
    active_f32, gelu_pull = jax.vjp(gelu_tanh, hidden_pre)
    active = active_f32.astype(jnp.bfloat16)
    partial_out = jnp.einsum(
        "rslcf,lfd->rslcd", active, expert_out, preferred_element_type=jnp.float32
    )
    result_rows = (
        lax.psum_scatter(partial_out.astype(jnp.bfloat16), "dp", scatter_dimension=0, tiled=True)
        .astype(jnp.float32)[0]
        .astype(jnp.bfloat16)
    )
    returned = lax.all_to_all(result_rows, "exp", split_axis=0, concat_axis=0, tiled=True)
    picked = jnp.take(
        returned.reshape(expert_count * capacity, model_width), slot_place, axis=0
    ).astype(jnp.float32)
    mixed = (middle + gate_prob * picked).astype(jnp.bfloat16)
    full_qkv, full_out, full_route = (
        lax.all_gather(attn_qkv, ("exp", "dp"), axis=0, tiled=True),
        lax.all_gather(attn_out, ("exp", "dp"), axis=0, tiled=True),
        lax.all_gather(router, ("exp", "dp"), axis=0, tiled=True),
    )
    grad_out = cotangent.astype(jnp.float32)
    grad_picked = (gate_prob * grad_out).astype(jnp.bfloat16)
    gate_grad = jnp.sum(grad_out * picked, axis=1, keepdims=True)
    logit_grad = (gate_probs * (jnp.where(choose, gate_grad, 0.0) - gate_prob * gate_grad)).astype(
        jnp.bfloat16
    )
    grad_slots = jnp.dot(dispatch, grad_picked, preferred_element_type=jnp.float32).astype(
        jnp.bfloat16
    )
    grad_slots = grad_slots.reshape(group_count, local_count, capacity, model_width)
    grad_arrived = lax.all_to_all(grad_slots, "exp", split_axis=0, concat_axis=0, tiled=True)
    grad_result = lax.all_gather(grad_arrived[None], "dp", axis=0, tiled=True)
    grad_active = jnp.einsum(
        "rslcd,lfd->rslcf", grad_result, expert_out, preferred_element_type=jnp.float32
    )
    grad_pre = gelu_pull(grad_active)[0].astype(jnp.bfloat16)
    grad_expert_out = jnp.einsum(
        "rslcf,rslcd->lfd", active, grad_result, preferred_element_type=jnp.float32
    )
    grad_expert_in = jnp.einsum(
        "rslcd,rslcf->ldf", expert_rows, grad_pre, preferred_element_type=jnp.float32
    )
    grad_part = jnp.einsum(
        "rslcf,ldf->rslcd", grad_pre, expert_in, preferred_element_type=jnp.float32
    )
    grad_rows = lax.psum_scatter(
        grad_part.astype(jnp.bfloat16), "dp", scatter_dimension=0, tiled=True
    ).astype(jnp.float32)[0]
    grad_back = lax.all_to_all(
        grad_rows.astype(jnp.bfloat16), "exp", split_axis=0, concat_axis=0, tiled=True
    ).astype(grad_rows.dtype)
    grad_ffn = jnp.take(grad_back.reshape(expert_count * capacity, model_width), slot_place, axis=0)
    grad_ffn = grad_ffn + jnp.dot(logit_grad, full_route.T, preferred_element_type=jnp.float32)
    grad_router = jnp.einsum("td,te->de", ffn_low, logit_grad, preferred_element_type=jnp.float32)
    grad_middle_norm, grad_gain_ffn = ffn_norm_pull(grad_ffn)
    grad_middle = grad_out + grad_middle_norm
    branch_grad = grad_middle.astype(jnp.bfloat16)
    grad_attn_out = jnp.einsum(
        "td,te->de", attended_low, branch_grad, preferred_element_type=jnp.float32
    )
    grad_attended = jnp.dot(branch_grad, full_out.T, preferred_element_type=jnp.float32).astype(
        jnp.bfloat16
    )
    grad_attended = grad_attended.reshape(row_count, head_count, head_size)
    scores = score_block(queries, key_rows, pos_bias, allowed, score_scale)
    attn_probs = jnp.exp(scores - log_total)
    grad_values = jnp.einsum(
        "hqk,qhe->khe",
        attn_probs.astype(jnp.bfloat16),
        grad_attended,
        preferred_element_type=jnp.float32,
    )
    grad_probs = jnp.einsum(
        "qhe,khe->hqk", grad_attended, value_rows, preferred_element_type=jnp.float32
    )
    inner_sum = jnp.sum(attn_probs * grad_probs, axis=-1, keepdims=True)
    grad_scores = (attn_probs * (grad_probs - inner_sum)).astype(jnp.bfloat16)
    grad_queries = (
        jnp.einsum("hqk,khe->qhe", grad_scores, key_rows, preferred_element_type=jnp.float32)
        * score_scale
    )
    grad_keys = (
        jnp.einsum("hqk,qhe->khe", grad_scores, queries, preferred_element_type=jnp.float32)
        * score_scale
    )
    bucket_hot = jnp.asarray(
        bucket_ids.reshape(-1)[:, None] == np.arange(bucket_count)[None, :], dtype=jnp.bfloat16
    )
    grad_bias = jnp.einsum(
        "nb,hn->bh",
        bucket_hot,
        grad_scores.reshape(head_count, row_count * row_count),
        preferred_element_type=jnp.float32,
    )
    grad_qkv = jnp.concatenate(
        [
            grad_queries.reshape(row_count, model_width),
            grad_keys.reshape(row_count, model_width),
            grad_values.reshape(row_count, model_width),
        ],
        axis=1,
    ).astype(jnp.bfloat16)
    grad_attn_qkv = jnp.einsum(
        "td,tf->df", normed_low, grad_qkv, preferred_element_type=jnp.float32
    )
    grad_normed = jnp.dot(grad_qkv, full_qkv.T, preferred_element_type=jnp.float32)
    grad_inputs_norm, grad_gain_attn = attn_norm_pull(grad_normed)
    grad_in = grad_middle + grad_inputs_norm
    stacked = jnp.concatenate([grad_attn_qkv, grad_attn_out, grad_router], axis=1)
    total_width = stacked.shape[1]
    dp_count = lax.axis_size("dp")
    shard_rows = model_width // (group_count * dp_count)
    pieces = lax.all_to_all(
        stacked.reshape(group_count, dp_count * shard_rows, total_width).astype(jnp.bfloat16),
        "exp",
        split_axis=0,
        concat_axis=0,
        tiled=True,
    ).astype(jnp.float32)
    partial_value = jnp.sum(pieces, axis=0).reshape(dp_count, shard_rows, total_width)
    pieces = lax.all_to_all(
        partial_value.astype(jnp.bfloat16), "dp", split_axis=0, concat_axis=0, tiled=True
    ).astype(partial_value.dtype)
    owned = jnp.sum(pieces, axis=0)
    grad_attn_qkv = owned[:, : 3 * model_width]
    grad_attn_out = owned[:, 3 * model_width : 4 * model_width]
    grad_router = owned[:, 4 * model_width :]
    grad_gain_attn, grad_gain_ffn, grad_bias = lax.psum(
        (grad_gain_attn, grad_gain_ffn, grad_bias), ("exp", "dp")
    )
    return (
        mixed,
        grad_in,
        grad_gain_attn,
        grad_attn_qkv,
        grad_attn_out,
        grad_bias,
        grad_gain_ffn,
        grad_router,
        grad_expert_in,
        grad_expert_out,
    )


def solution(mesh):
    return jax.shard_map(
        local,
        mesh=mesh,
        in_specs=(
            P(("exp", "dp"), None),
            P(("exp", "dp"), None),
            P(("exp", "dp"), None),
            P(("exp", "dp"), None),
            P(),
            P(("exp", "dp"), None),
            P(("exp", "dp"), None),
            P(),
            P(),
            P(("exp", "dp"), None),
            P("exp", None, "dp"),
            P("exp", "dp", None),
        ),
        out_specs=(
            P(("exp", "dp"), None),
            P(("exp", "dp"), None),
            P(),
            P(("exp", "dp"), None),
            P(("exp", "dp"), None),
            P(),
            P(),
            P(("exp", "dp"), None),
            P("exp", None, "dp"),
            P("exp", "dp", None),
        ),
        check_vma=False,
    )
```

profile of v0, /device:TPU:0, one launch (start us, length us, event | category | flops | bytes accessed | tf_op | source)
XLA Modules:
  0.0 419.5 jit_solution(2512068221017108920)
XLA Ops:
  7.2 0.7 all-gather.6.cloned.1.call-update
  8.0 0.7 all-gather.8.cloned.1.call-update
  8.7 0.8 copy.136
  9.5 0.8 broadcast_clamp_fusion
  10.3 54.8 %gather_fusion = f32[16384,12]{1,0:T(8,128)} fusion(f32[32,12]{1,0:T(8,128)S(1)} %copy.136, s32[16384]{0:T(1024)S(1)} %broadcast_clamp_fusion), kind=kCustom, calls=%fused_computation | custom fusion | bytes 1638400 | tf_op jit(solution)/shard_map/jit(_take)/gather | solution.py:86
  65.1 7.6 %copy.138 = f32[128,128,12]{0,1,2:T(8,128)} copy(f32[128,128,12]{2,1,0:T(8,128)} %bitcast.134) | data formatting | bytes 1572864 | tf_op jit(solution)/shard_map/jit(_take)/gather | solution.py:86
  73.3 70.9 %all-gather.2 = bf16[32,24,16]{1,2,0:T(8,128)(2,1)S(1)} all-gather(bf16[1,24,16]{1,2,0:T(8,128)(2,1)S(1)} %bitcast.165), channel_id=1, replica_groups=mesh['exp'=8,'dp'=4] {'exp','dp'}, dimensions={0}, use_global_device_ids=true | all-gather | bytes 25344 | tf_op jit(solution)/shard_map/all_gather | solution.py:76
  144.3 0.8 reshape.267
  145.9 2.7 convolution_convert_fusion.1
  148.6 0.8 copy.133
  149.6 0.8 copy.135
  150.4 1.6 fusion.80
  152.5 1.8 multiply_reduce_fusion.3
  154.4 0.7 copy-done.5
  155.2 0.9 convolution_convert_fusion.4
  156.1 1.8 reshape.227
  157.9 1.9 copy.143
  159.8 4.0 all-to-all-start
  163.9 1.4 fusion.81
  165.3 5.3 %all-to-all-done = bf16[8,2,10,768]{3,1,2,0:T(2,128)(2,1)} async-done(((bf16[8,2,10,768]{3,1,2,0:T(2,128)(2,1)}), bf16[8,2,10,768]{3,1,2,0:T(2,128)(2,1)}, u32[]{:S(2)}, u32[]{:S(2)}) %all-to-all-start) | async-done | bytes 245792 | tf_op jit(solution)/shard_map/all_to_all | solution.py:116
  170.6 20.0 %all-gather = bf16[32,2,10,768]{3,1,2,0:T(2,128)(2,1)S(1)} all-gather(bf16[8,2,10,768]{3,1,2,0:T(2,128)(2,1)} %all-to-all-done), channel_id=2, replica_groups=mesh['exp'=8,'dp'=4] {'dp'}, dimensions={0}, use_global_device_ids=true | all-gather | bytes 1228800 | tf_op jit(solution)/shard_map/all_gather | solution.py:117
  190.8 2.4 fusion.18
  193.4 1.4 fusion.36
  194.8 1.3 copy.147
  196.2 0.7 fusion.73
  196.9 0.6 copy-done.34
  197.4 0.7 select_reduce_fusion.1
  198.6 1.9 convolution_convert_fusion.3
  200.5 1.8 reshape.229
  202.3 1.3 copy.150
  203.6 9.2 %all_to_all.30 = bf16[8,2,10,768]{3,1,2,0:T(2,128)(2,1)S(1)} all-to-all(bf16[8,2,10,768]{3,1,2,0:T(2,128)(2,1)S(1)} %copy.150), channel_id=1, replica_groups=mesh['exp'=8,'dp'=4] {'exp'}, dimensions={0} | all-to-all | bytes 491520 | tf_op jit(solution)/shard_map/all_to_all | solution.py:151
  212.8 22.6 %all-gather.1 = bf16[32,2,10,768]{3,1,2,0:T(2,128)(2,1)S(1)} all-gather(bf16[8,2,10,768]{3,1,2,0:T(2,128)(2,1)S(1)} %all_to_all.30), channel_id=3, replica_groups=mesh['exp'=8,'dp'=4] {'dp'}, dimensions={0}, use_global_device_ids=true | all-gather | bytes 1228800 | tf_op jit(solution)/shard_map/all_gather | solution.py:152
  235.6 1.9 fusion.14
  237.6 1.4 fusion.31
  239.1 1.3 copy.154
  240.4 1.8 copy.148
  242.2 3.6 all-to-all-start.1
  245.9 19.2 %reduce-scatter.5.cloned.1.call-done = bf16[1,8,2,10,768]{4,1,3,2,0:T(8,128)(2,1)} async-done(((bf16[4,8,2,10,768]{4,1,3,2,0:T(8,128)(2,1)}), bf16[1,8,2,10,768]{4,1,3,2,0:T(8,128)(2,1)}) %reduce-scatter.5.cloned.1.call-update) | async-done | bytes 245776 | tf_op jit(solution)/shard_map/reduce_scatter | solution.py:166
  265.1 1.9 copy.155
  267.0 3.8 all-to-all-start.3
  270.9 0.9 gather_fusion.1
  272.6 4.9 %all-to-all-done.3 = bf16[8,2,10,768]{3,1,2,0:T(2,128)(2,1)S(1)} async-done(((bf16[8,2,10,768]{3,1,2,0:T(2,128)(2,1)}), bf16[8,2,10,768]{3,1,2,0:T(2,128)(2,1)S(1)}, u32[]{:S(2)}, u32[]{:S(2)}) %all-to-all-start.3) | async-done | bytes 245792 | tf_op jit(solution)/shard_map/all_to_all | solution.py:169
  277.9 1.8 gather_fusion.2
  279.7 2.1 multiply_reduce_fusion.1
  281.8 0.6 multiply_multiply_fusion.3
  282.4 1.6 convert_add_fusion
  284.0 0.5 convolution_convert_fusion.6
  284.8 1.1 convolution_convert_fusion.5
  288.3 1.2 convolution_convert_fusion
  289.5 2.4 pad_maximum_fusion
  291.9 5.0 %all-to-all-start.4 = ((bf16[8,96,3088]{2,1,0:T(8,128)(2,1)}), bf16[8,96,3088]{2,1,0:T(8,128)(2,1)}, u32[]{:S(2)}, u32[]{:S(2)}) async-start(bf16[8,96,3088]{2,1,0:T(8,128)(2,1)} %bitcast.135), calls=%async_computation.6 | async-start | bytes 9830400 | tf_op jit(solution)/shard_map/all_to_all | solution.py:233
  296.9 5.1 %convolution_bitcast_fusion = f32[2,768,768]{2,1,0:T(8,128)} fusion(bf16[4,8,2,10,768]{4,1,3,2,0:T(8,128)(2,1)} %copy-done.58, bf16[4,8,2,10,768]{4,3,1,0,2:T(8,128)(2,1)S(1)} %bitcast.149), kind=kOutput, calls=%fused_computation.16 | convolution fusion | flops 754974720 | bytes 6684672 | tf_op jit(solution)/shard_map/rslcd,rslcf->ldf/dot_general | solution.py:160
  302.1 3.7 convolution_bitcast_fusion.1
  306.4 47.1 %all-to-all-done.4 = bf16[8,96,3088]{2,1,0:T(8,128)(2,1)} async-done(((bf16[8,96,3088]{2,1,0:T(8,128)(2,1)}), bf16[8,96,3088]{2,1,0:T(8,128)(2,1)}, u32[]{:S(2)}, u32[]{:S(2)}) %all-to-all-start.4) | async-done | bytes 4743200 | tf_op jit(solution)/shard_map/all_to_all | solution.py:233
  353.5 4.1 reduce_sum.169
  357.7 4.3 %all-to-all-start.5 = ((bf16[4,24,3088]{2,1,0:T(8,128)(2,1)}), bf16[4,24,3088]{2,1,0:T(8,128)(2,1)}, u32[]{:S(2)}, u32[]{:S(2)}) async-start(bf16[4,24,3088]{2,1,0:T(8,128)(2,1)} %bitcast.36), calls=%async_computation.7 | async-start | bytes 1228800 | tf_op jit(solution)/shard_map/all_to_all | solution.py:241
  362.4 4.8 %fusion.52 = (f32[768]{0:T(1024)}, f32[128]{0:T(128)}, f32[128,768]{1,0:T(8,128)}) fusion(bf16[128,768]{1,0:T(8,128)(2,1)S(1)} %copy-done.2, f32[128]{0:T(128)} %copy-done.37, f32[768]{0:T(1024)S(1)} %copy-done.27, bf16[768,2304]{1,0:T(8,128)(2,1)} %all-gather.6.cloned.1.call-done, bf16[128,768]{0,1:T(8,128)(2,1)S(1)} %bitcast.153, ...), kind=kOutput, calls=%fused_computation.79 | convolution fusion | flops 455441536 | bytes 4725760 | tf_op jit(solution)/shard_map/dot_general | solution.py:226
  367.2 40.0 %all-reduce = (f32[768]{0:T(1024)}, f32[32,12]{0,1:T(8,128)}, f32[768]{0:T(1024)}) all-reduce(f32[768]{0:T(1024)} %get-tuple-element.62, f32[32,12]{0,1:T(8,128)S(1)} %fusion.82, f32[768]{0:T(1024)S(1)} %copy-done.32), channel_id=1, replica_groups=mesh['exp'=8,'dp'=4] {'exp','dp'}, use_global_device_ids=true, to_apply=%region_18.19 | all-reduce | flops 1920 | bytes 15360 | tf_op jit(solution)/shard_map/psum | solution.py:248
  407.2 0.7 multiply_multiply_fusion.2
  407.9 1.9 fusion.57
  409.8 1.2 convert_reduce_fusion
  411.0 0.7 slice.33
  411.7 0.6 slice.34
  412.3 0.7 copy.169
  (170 shorter events, 8.2 us)
Async XLA Ops:
  7.2 183.6 %copy-start = (bf16[2,768,768]{2,1,0:T(8,128)(2,1)S(1)}, bf16[2,768,768]{2,1,0:T(8,128)(2,1)}, u32[]{:S(2)}) copy-start(bf16[2,768,768]{2,1,0:T(8,128)(2,1)} %param.24) | copy-start | bytes 7077892
  7.2 138.7 %all-gather.6.cloned.1.call-start = ((), (), s32[]{:S(2)}) async-start(), calls=%async_computation.8 | async-start | bytes 3649536 | tf_op jit(solution)/shard_map/all_gather | solution.py:74
  7.9 144.6 %all-gather.8.cloned.1.call-start = ((), (), s32[]{:S(2)}) async-start(), calls=%async_computation.9 | async-start | bytes 1216512 | tf_op jit(solution)/shard_map/all_gather | solution.py:75
  65.1 7.6 %copy-start.54 = (s32[1,3]{1,0:T(1,128)S(1)}, s32[1,3]{1,0:T(1,128)}, u32[]{:S(2)}) copy-start(s32[1,3]{1,0:T(1,128)} %param.16) | copy-start | bytes 40
  65.1 7.9 %copy-start.29 = (s32[128,1]{0,1:T(1,128)S(1)}, s32[128,1]{0,1:T(1,128)}, u32[]{:S(2)}) copy-start(s32[128,1]{0,1:T(1,128)} %param.17) | copy-start | bytes 1540
  65.1 8.3 %copy-start.45 = (bf16[24,16]{0,1:T(8,128)(2,1)S(1)}, bf16[24,16]{0,1:T(8,128)(2,1)}, u32[]{:S(2)}) copy-start(bf16[24,16]{0,1:T(8,128)(2,1)} %param.23) | copy-start | bytes 2308
  65.1 80.0 %copy-start.2 = (bf16[128,768]{1,0:T(8,128)(2,1)S(1)}, bf16[128,768]{1,0:T(8,128)(2,1)}, u32[]{:S(2)}) copy-start(bf16[128,768]{1,0:T(8,128)(2,1)} %param.14) | copy-start | bytes 589828
  65.1 80.8 %copy-start.26 = (f32[768]{0:T(1024)S(1)}, f32[768]{0:T(1024)}, u32[]{:S(2)}) copy-start(f32[768]{0:T(1024)} %param.18) | copy-start | bytes 9220
  73.3 72.5 %copy-start.47 = (s32[128]{0:T(128)}, s32[128]{0:T(128)S(1)}, u32[]{:S(2)}) copy-start(s32[128]{0:T(128)S(1)} %select_reduce_fusion) | copy-start | bytes 1540
  149.6 2.6 copy-start.15
  150.4 1.8 copy-start.11
  152.1 3.0 copy-start.28
  152.2 3.0 copy-start.49
  152.5 1.9 copy-start.8
  154.3 0.8 copy-start.5
  154.3 0.9 copy-start.51
  154.4 0.8 copy-start.44
  159.8 10.8 %all-to-all-start = ((bf16[8,2,10,768]{3,1,2,0:T(2,128)(2,1)}), bf16[8,2,10,768]{3,1,2,0:T(2,128)(2,1)}, u32[]{:S(2)}, u32[]{:S(2)}) async-start(bf16[8,2,10,768]{3,1,2,0:T(2,128)(2,1)} %copy.143), calls=%async_computation | async-start | bytes 491520 | tf_op jit(solution)/shard_map/all_to_all | solution.py:116
  163.8 76.5 %reduce-scatter.3.cloned.1.call-start = ((), (), s32[]{:S(2)}) async-start(), calls=%async_computation.10 | async-start | bytes 1228800 | tf_op jit(solution)/shard_map/reduce_scatter | solution.py:127
  190.8 2.4 copy-start.18
  190.8 2.6 copy-start.52
  193.2 1.6 copy-start.56
  196.1 69.0 %reduce-scatter.5.cloned.1.call-start = ((), (), s32[]{:S(2)}) async-start(), calls=%async_computation.11 | async-start | bytes 1228800 | tf_op jit(solution)/shard_map/reduce_scatter | solution.py:166
  202.3 33.3 %copy-start.55 = (f32[2,4,8,10,768]{4,2,3,0,1:T(8,128)S(1)}, f32[2,4,8,10,768]{4,2,3,0,1:T(8,128)}, u32[]{:S(2)}) copy-start(f32[2,4,8,10,768]{4,2,3,0,1:T(8,128)} %get-tuple-element.81) | copy-start | bytes 5898244
  212.8 22.8 %copy-start.53 = (bf16[2,768,768]{2,1,0:T(8,128)(2,1)S(1)}, bf16[2,768,768]{2,1,0:T(8,128)(2,1)}, u32[]{:S(2)}) copy-start(bf16[2,768,768]{2,1,0:T(8,128)(2,1)} %param.25) | copy-start | bytes 7077892
  235.6 2.0 copy-start.20
  237.6 1.4 copy-start.58
  239.0 6.8 %copy-start.30 = (s32[128,1]{0,1:T(1,128)S(1)}, s32[128,1]{0,1:T(1,128)}, u32[]{:S(2)}) copy-start(s32[128,1]{0,1:T(1,128)} %param.17) | copy-start | bytes 1540
  239.0 6.8 %copy-start.48 = (s32[128]{0:T(128)S(1)}, s32[128]{0:T(128)}, u32[]{:S(2)}) copy-start(s32[128]{0:T(128)} %copy-done.47) | copy-start | bytes 1540
  242.2 24.8 %all-to-all-start.1 = ((bf16[8,2,10,768]{3,1,2,0:T(2,128)(2,1)}), bf16[8,2,10,768]{3,1,2,0:T(2,128)(2,1)S(1)}, u32[]{:S(2)}, u32[]{:S(2)}) async-start(bf16[8,2,10,768]{3,1,2,0:T(2,128)(2,1)} %copy.148), calls=%async_computation.2 | async-start | bytes 491520 | tf_op jit(solution)/shard_map/all_to_all | solution.py:131
  245.9 26.0 %copy-start.36 = (pred[128]{0:T(512)(128)(4,1)}, pred[128]{0:T(512)(128)(4,1)S(1)}, u32[]{:S(2)}) copy-start(pred[128]{0:T(512)(128)(4,1)S(1)} %get-tuple-element.67) | copy-start | bytes 388
  265.1 6.7 %copy-start.10 = (bf16[128,768]{1,0:T(8,128)(2,1)S(1)}, bf16[128,768]{1,0:T(8,128)(2,1)}, u32[]{:S(2)}) copy-start(bf16[128,768]{1,0:T(8,128)(2,1)} %param.15) | copy-start | bytes 589828
  267.0 5.1 %copy-start.43 = (f32[128]{0:T(128)S(1)}, f32[128]{0:T(128)}, u32[]{:S(2)}) copy-start(f32[128]{0:T(128)} %copy-done.42) | copy-start | bytes 1540
  267.0 10.6 %all-to-all-start.3 = ((bf16[8,2,10,768]{3,1,2,0:T(2,128)(2,1)}), bf16[8,2,10,768]{3,1,2,0:T(2,128)(2,1)S(1)}, u32[]{:S(2)}, u32[]{:S(2)}) async-start(bf16[8,2,10,768]{3,1,2,0:T(2,128)(2,1)} %copy.155), calls=%async_computation.5 | async-start | bytes 491520 | tf_op jit(solution)/shard_map/all_to_all | solution.py:169
  270.8 6.8 %copy-start.39 = (s32[1024]{0:T(1024)}, s32[1024]{0:T(1024)S(1)}, u32[]{:S(2)}) copy-start(s32[1024]{0:T(1024)S(1)} %pad_clamp_fusion) | copy-start | bytes 12292
  271.8 5.8 %copy-start.13 = (bf16[128,768]{1,0:T(8,128)(2,1)}, bf16[128,768]{1,0:T(8,128)(2,1)S(1)}, u32[]{:S(2)}) copy-start(bf16[128,768]{1,0:T(8,128)(2,1)S(1)} %gather_fusion.1) | copy-start | bytes 589828
  272.0 5.5 %copy-start.40 = (f32[128]{0:T(128)}, f32[128]{0:T(128)S(1)}, u32[]{:S(2)}) copy-start(f32[128]{0:T(128)S(1)} %fusion.56) | copy-start | bytes 1540
  277.8 1.8 copy-start.6
  277.8 4.6 %copy-start.14 = (bf16[128,768]{1,0:T(8,128)(2,1)S(1)}, bf16[128,768]{1,0:T(8,128)(2,1)}, u32[]{:S(2)}) copy-start(bf16[128,768]{1,0:T(8,128)(2,1)} %copy-done.13) | copy-start | bytes 589828
  279.7 4.4 %copy-start.7 = (bf16[768,768]{1,0:T(8,128)(2,1)S(1)}, bf16[768,768]{1,0:T(8,128)(2,1)}, u32[]{:S(2)}) copy-start(bf16[768,768]{1,0:T(8,128)(2,1)} %all-gather.8.cloned.1.call-done) | copy-start | bytes 3538948
  284.0 3.5 copy-start.3
  284.0 1.8 copy-start.12
  285.8 0.9 copy-start.16
  285.8 1.3 copy-start.17
  286.2 1.2 copy-start.31
  286.2 1.2 copy-start.33
  286.2 1.2 copy-start.35
  286.2 1.2 copy-start.41
  286.2 1.2 copy-start.46
  286.2 1.4 copy-start.9
  286.8 1.5 copy-start.23
  286.8 1.5 copy-start.27
  286.8 1.5 copy-start.38
  287.4 2.0 copy-start.24
  291.9 5.0 %copy-start.19 = (bf16[32,2,10,768]{3,2,0,1:T(8,128)(2,1)S(1)}, bf16[32,2,10,768]{3,2,0,1:T(8,128)(2,1)}, u32[]{:S(2)}) copy-start(bf16[32,2,10,768]{3,2,0,1:T(8,128)(2,1)} %copy-done.18) | copy-start | bytes 2949124
  291.9 61.6 %all-to-all-start.4 = ((bf16[8,96,3088]{2,1,0:T(8,128)(2,1)}), bf16[8,96,3088]{2,1,0:T(8,128)(2,1)}, u32[]{:S(2)}, u32[]{:S(2)}) async-start(bf16[8,96,3088]{2,1,0:T(8,128)(2,1)} %bitcast.135), calls=%async_computation.6 | async-start | bytes 9830400 | tf_op jit(solution)/shard_map/all_to_all | solution.py:233
  296.9 5.2 %copy-start.21 = (bf16[32,2,10,768]{3,2,0,1:T(8,128)(2,1)S(1)}, bf16[32,2,10,768]{3,2,0,1:T(8,128)(2,1)}, u32[]{:S(2)}) copy-start(bf16[32,2,10,768]{3,2,0,1:T(8,128)(2,1)} %copy-done.20) | copy-start | bytes 2949124
  296.9 5.2 %copy-start.57 = (bf16[4,8,2,10,768]{4,1,3,2,0:T(8,128)(2,1)S(1)}, bf16[4,8,2,10,768]{4,1,3,2,0:T(8,128)(2,1)}, u32[]{:S(2)}) copy-start(bf16[4,8,2,10,768]{4,1,3,2,0:T(8,128)(2,1)} %copy-done.56) | copy-start | bytes 2949124
  306.4 55.6 %copy-start.22 = (bf16[16384,32]{0,1:T(8,128)(2,1)S(1)}, bf16[16384,32]{0,1:T(8,128)(2,1)}, u32[]{:S(2)}) copy-start(bf16[16384,32]{0,1:T(8,128)(2,1)} %constant.94.clone) | copy-start | bytes 3145732
  357.7 4.7 %copy-start.25 = (bf16[12,64,128]{2,1,0:T(8,128)(2,1)S(1)}, bf16[12,64,128]{2,1,0:T(8,128)(2,1)}, u32[]{:S(2)}) copy-start(bf16[12,64,128]{2,1,0:T(8,128)(2,1)} %copy-done.24) | copy-start | bytes 589828
  357.7 52.1 %all-to-all-start.5 = ((bf16[4,24,3088]{2,1,0:T(8,128)(2,1)}), bf16[4,24,3088]{2,1,0:T(8,128)(2,1)}, u32[]{:S(2)}, u32[]{:S(2)}) async-start(bf16[4,24,3088]{2,1,0:T(8,128)(2,1)} %bitcast.36), calls=%async_computation.7 | async-start | bytes 1228800 | tf_op jit(solution)/shard_map/all_to_all | solution.py:241
  362.4 4.8 %copy-start.32 = (f32[768]{0:T(1024)S(1)}, f32[768]{0:T(1024)}, u32[]{:S(2)}) copy-start(f32[768]{0:T(1024)} %get-tuple-element.60) | copy-start | bytes 9220
  362.4 45.5 %copy-start.4 = (f32[128,768]{1,0:T(8,128)S(1)}, f32[128,768]{1,0:T(8,128)}, u32[]{:S(2)}) copy-start(f32[128,768]{1,0:T(8,128)} %copy-done.3) | copy-start | bytes 1179652
  362.4 50.6 %copy-start.1 = (bf16[2,768,768]{2,1,0:T(8,128)(2,1)S(1)}, bf16[2,768,768]{2,1,0:T(8,128)(2,1)}, u32[]{:S(2)}) copy-start(bf16[2,768,768]{2,1,0:T(8,128)(2,1)} %param.24) | copy-start | bytes 7077892
  (4 other events, 2.4 us)
Sparse Core Ops, SparseCore 0:
  10.8 62.8 all-gather.5
  76.5 52.9 all-gather.7
  196.2 25.4 reduce-scatter.2
  240.4 24.5 reduce-scatter.4
where the time goes:
time: 421 us; the launch traced here: 420 us
  blocking collectives  163 us (39%)
  local copies, waits for them, and re-layouts  87.9 us (21%)
  waiting for transfers between devices  78 us (19%)
  matrix products  38.2 us (9%)
  starting transfers between devices  20.9 us (5%)
  other arithmetic  17.2 us (4%)
  between operations  14.7 us (3%)
    all_gather x1, blocking collectives, local(): lax.all_gather(router, ('exp', 'dp'), axis=0, tiled=True)  70.9 us
    gather x2, local copies, waits for them, and re-layouts, local(): pos_bias = jnp.transpose(jnp.take(rel_bias, bucket_ids, axis=0), (2, 0, 1))  62.3 us
    all_to_all x1, waiting for transfers between devices, local(): lax.all_to_all(stacked.reshape(group_count, dp_count * shard_rows, total_...  47.1 us
    psum x1, blocking collectives, local(): lax.psum((grad_gain_attn, grad_gain_ffn, grad_bias), ('exp', 'dp'))  40 us
    all_gather x1, blocking collectives, local(): grad_result = lax.all_gather(grad_arrived[None], 'dp', axis=0, tiled=True)  22.6 us
    all_gather x1, blocking collectives, local(): expert_rows = lax.all_gather(arrived[None], 'dp', axis=0, tiled=True)  20 us
    reduce_scatter x1, waiting for transfers between devices, local(): lax.psum_scatter(grad_part.astype(jnp.bfloat16), 'dp', scatter_dimension=...  19.2 us
    all_to_all x1, blocking collectives, local(): lax.all_to_all(grad_slots, 'exp', split_axis=0, concat_axis=0, tiled=True)  9.17 us
  transfers between devices with their start and end apart: 9, of which 4 were waited for; matrix products, arithmetic and copies ran while one was open for 26% of the time, Pallas kernels for 0%

commit v1 on v0

--- a/solution.py
+++ b/solution.py
@@ -1,8 +1,16 @@
+import functools
+
 import jax
 import jax.numpy as jnp
 import numpy as np
 from jax import lax
+from jax.experimental import pallas as pl
+from jax.experimental.pallas import tpu as pltpu
 from jax.sharding import PartitionSpec as P
+
+MESH = pl.DeviceIdType.MESH
+lane_count = 128
+by_y = (0, 3)
 
 epsilon = 1e-06
 
@@ -46,6 +54,255 @@
         + pos_bias
     )
     return jnp.where(allowed, scores, -1e30)
+
+
+def positions():
+    e, z = lax.axis_index("exp"), lax.axis_index("dp")
+    core, side_x, side_y = lax.rem(e, 2), lax.rem(lax.div(e, 2), 2), lax.div(e, 4)
+    step_core, step_x, step_y = 1 - 2 * core, 2 - 4 * side_x, 4 - 8 * side_y
+    chips = (e, e + step_x, e + step_y, e + step_x + step_y)
+    return e, z, step_core, chips
+
+
+def greet(devices):
+    barrier = pltpu.get_barrier_semaphore()
+    for device in devices:
+        pl.semaphore_signal(barrier, inc=1, device_id=device, device_id_type=MESH)
+    pl.semaphore_wait(barrier, len(devices))
+
+
+def gather_kernel(mine_ref, full_ref, local_sem, send_sem, recv_sem):
+    e, z, step_core, chips = positions()
+    zs = [lax.rem(z + j, 4) for j in range(4)]
+    partner = (e + step_core, z)
+    beside = {1: (chips[1], z), 2: (chips[2], z)}
+    along = {j: (e, zs[j]) for j in (1, 2, 3)}
+    greet([partner, beside[1], beside[2], along[1], along[2], along[3]])
+    sends = []
+
+    def send(src, chip, j, device, recv):
+        copy = pltpu.make_async_remote_copy(
+            src_ref=src,
+            dst_ref=full_ref.at[chips[chip] * 4 + zs[j]],
+            send_sem=send_sem.at[len(sends)],
+            recv_sem=recv_sem.at[recv],
+            device_id=device,
+            device_id_type=MESH,
+        )
+        copy.start()
+        sends.append(copy)
+
+    def held(chip, j):
+        return full_ref.at[chips[chip] * 4 + zs[j]]
+
+    def arrive(place, recv):
+        pltpu.make_async_remote_copy(
+            src_ref=place,
+            dst_ref=place,
+            send_sem=send_sem.at[0],
+            recv_sem=recv_sem.at[recv],
+            device_id=partner,
+            device_id_type=MESH,
+        ).wait_recv()
+
+    def spread(src, j):
+        send(src, 0, j, beside[1], 4 + j)
+        send(src, 0, j, beside[2], 8 + j)
+        send(src, 0, j, partner, 16 + j)
+
+    def from_x(j):
+        arrive(held(1, j), 4 + j)
+        if j in by_y:
+            send(held(1, j), 1, j, beside[2], 12 + j)
+        send(held(1, j), 1, j, partner, 20 + j)
+
+    def from_y(j):
+        arrive(held(2, j), 8 + j)
+        if j not in by_y:
+            send(held(2, j), 2, j, beside[1], 12 + j)
+        send(held(2, j), 2, j, partner, 24 + j)
+
+    own = pltpu.make_async_copy(mine_ref, held(0, 0), local_sem)
+    own.start()
+    for j in (1, 3, 2):
+        send(mine_ref, 0, 0, along[j], (4 - j) % 4)
+    spread(mine_ref, 0)
+    for j in (3, 1):
+        arrive(held(0, j), j)
+        spread(held(0, j), j)
+    from_x(0)
+    from_y(0)
+    arrive(held(0, 2), 2)
+    spread(held(0, 2), 2)
+    for j in (3, 1, 2):
+        from_x(j)
+        from_y(j)
+    for j in (0, 3, 1, 2):
+        arrive(held(3, j), 12 + j)
+        send(held(3, j), 3, j, partner, 28 + j)
+    for chip in range(4):
+        for j in range(4):
+            arrive(full_ref.at[(chips[chip] + step_core) * 4 + zs[j]], 16 + chip * 4 + j)
+    for copy in sends:
+        copy.wait_send()
+    own.wait()
+
+
+def gather_rows(mine):
+    rows, width = mine.shape
+    full = pl.pallas_call(
+        gather_kernel,
+        out_shape=jax.ShapeDtypeStruct((32, rows, width), mine.dtype),
+        in_specs=[pl.BlockSpec(memory_space=pl.ANY)],
+        out_specs=pl.BlockSpec(memory_space=pl.ANY),
+        scratch_shapes=[
+            pltpu.SemaphoreType.DMA,
+            pltpu.SemaphoreType.DMA((31,)),
+            pltpu.SemaphoreType.DMA((32,)),
+        ],
+        compiler_params=pltpu.CompilerParams(collective_id=0, has_side_effects=True),
+        cost_estimate=pl.CostEstimate(flops=0, bytes_accessed=64 * rows * width, transcendentals=0),
+        name="gather_rows",
+    )(mine)
+    return full.reshape(32 * rows, width)
+
+
+def reduce_kernel(
+    grad_ref, small_ref, out_ref, total_ref,
+    from_core, summed, passing, from_x, from_y, from_z,
+    small_sum, small_in, small_z, send_sem, recv_sem, small_send, small_recv,
+):
+    e, z, step_core, chips = positions()
+    zs = [lax.rem(z + j, 4) for j in range(4)]
+    partner = (e + step_core, z)
+    beside = {1: (chips[1], z), 2: (chips[2], z)}
+    along = {j: (e, zs[j]) for j in (1, 2, 3)}
+    greet([partner, beside[1], beside[2], along[1], along[2], along[3]])
+    sends = []
+
+    def send(src, dst, device, recv):
+        copy = pltpu.make_async_remote_copy(
+            src_ref=src,
+            dst_ref=dst,
+            send_sem=send_sem.at[len(sends)],
+            recv_sem=recv_sem.at[recv],
+            device_id=device,
+            device_id_type=MESH,
+        )
+        copy.start()
+        sends.append(copy)
+
+    def small_copy(src, dst, device, number, recv):
+        return pltpu.make_async_remote_copy(
+            src_ref=src,
+            dst_ref=dst,
+            send_sem=small_send.at[number],
+            recv_sem=small_recv.at[recv],
+            device_id=device,
+            device_id_type=MESH,
+        )
+
+    def arrive(place, recv):
+        pltpu.make_async_remote_copy(
+            src_ref=place,
+            dst_ref=place,
+            send_sem=send_sem.at[0],
+            recv_sem=recv_sem.at[recv],
+            device_id=partner,
+            device_id_type=MESH,
+        ).wait_recv()
+        return place[...].astype(jnp.float32)
+
+    def pair(chip, j):
+        number = chip * 4 + j
+        mine = grad_ref[chips[chip] * 4 + zs[j]].astype(jnp.float32)
+        return mine + arrive(from_core.at[number], number)
+
+    def step_sum(number, device):
+        copy = small_copy(small_sum.at[number], small_in.at[number], device, number, number)
+        copy.start()
+        copy.wait_recv()
+        small_sum[number + 1] = small_sum[number] + small_in[number]
+        return copy
+
+    small_sum[0] = small_ref[...]
+    for chip in (3, 1, 2, 0):
+        for j in (0, 1, 3, 2):
+            place = (chips[chip] + step_core) * 4 + zs[j]
+            send(grad_ref.at[place], from_core.at[chip * 4 + j], partner, chip * 4 + j)
+    small_copies = [step_sum(0, partner)]
+    for j in (0, 1, 3, 2):
+        number = 12 + j
+        summed[number] = pair(3, j).astype(jnp.bfloat16)
+        device = beside[2] if j in by_y else beside[1]
+        send(summed.at[number], passing.at[j], device, 16 + j)
+    small_copies.append(step_sum(1, beside[1]))
+    for j, chip in ((1, 1), (0, 2), (2, 1), (3, 2), (0, 1), (1, 2), (3, 1), (2, 2)):
+        number = chip * 4 + j
+        value = pair(chip, j)
+        if (j in by_y) == (chip == 1):
+            value = value + arrive(passing.at[j], 16 + j)
+        summed[number] = value.astype(jnp.bfloat16)
+        landing = from_x if chip == 1 else from_y
+        send(summed.at[number], landing.at[j], beside[chip], 16 + number)
+    small_copies.append(step_sum(2, beside[2]))
+    small_z[0] = small_sum[3]
+    for j in (1, 2, 3):
+        copy = small_copy(small_z.at[0], small_z.at[4 - j], along[j], 2 + j, 6 - j)
+        copy.start()
+        small_copies.append(copy)
+    for j in (1, 2, 3, 0):
+        value = pair(0, j) + arrive(from_x.at[j], 20 + j) + arrive(from_y.at[j], 24 + j)
+        if j == 0:
+            for other in (1, 2, 3):
+                value = value + arrive(from_z.at[other - 1], 27 + other)
+            out_ref[...] = value
+        else:
+            summed[j] = value.astype(jnp.bfloat16)
+            send(summed.at[j], from_z.at[3 - j], along[j], 31 - j)
+    for copy in small_copies[3:]:
+        copy.wait_recv()
+    spot = [lax.rem(4 + k - z, 4) for k in range(4)]
+    total_ref[...] = (small_z[spot[0]] + small_z[spot[1]]) + (small_z[spot[2]] + small_z[spot[3]])
+    for copy in sends + small_copies:
+        copy.wait_send()
+
+
+def reduce_rows(grads, small):
+    _, rows, width = grads.shape
+    vmem = pl.BlockSpec(memory_space=pltpu.VMEM)
+    block = functools.partial(pltpu.VMEM, dtype=jnp.bfloat16)
+    return pl.pallas_call(
+        reduce_kernel,
+        out_shape=(
+            jax.ShapeDtypeStruct((rows, width), jnp.float32),
+            jax.ShapeDtypeStruct(small.shape, jnp.float32),
+        ),
+        in_specs=[vmem, vmem],
+        out_specs=(vmem, vmem),
+        scratch_shapes=[
+            block((16, rows, width)),
+            block((16, rows, width)),
+            block((4, rows, width)),
+            block((4, rows, width)),
+            block((4, rows, width)),
+            block((3, rows, width)),
+            pltpu.VMEM((4,) + small.shape, jnp.float32),
+            pltpu.VMEM((3,) + small.shape, jnp.float32),
+            pltpu.VMEM((4,) + small.shape, jnp.float32),
+            pltpu.SemaphoreType.DMA((31,)),
+            pltpu.SemaphoreType.DMA((31,)),
+            pltpu.SemaphoreType.DMA((6,)),
+            pltpu.SemaphoreType.DMA((6,)),
+        ],
+        compiler_params=pltpu.CompilerParams(
+            collective_id=1, has_side_effects=True, vmem_limit_bytes=40 * 1024 * 1024
+        ),
+        cost_estimate=pl.CostEstimate(
+            flops=64 * rows * width, bytes_accessed=64 * rows * width, transcendentals=0
+        ),
+        name="reduce_rows",
+    )(grads, small)
 
 
 def local(
@@ -70,11 +327,27 @@
     group_count = lax.axis_size("exp")
     local_count = expert_in.shape[0]
     capacity = max(2, row_count * 5 // (4 * expert_count))
-    full_qkv, full_out, full_route = (
-        lax.all_gather(attn_qkv, ("exp", "dp"), axis=0, tiled=True),
-        lax.all_gather(attn_out, ("exp", "dp"), axis=0, tiled=True),
-        lax.all_gather(router, ("exp", "dp"), axis=0, tiled=True),
-    )
+    dp_count = lax.axis_size("dp")
+    shard_rows = attn_qkv.shape[0]
+    direct = group_count == 8 and dp_count == 4 and shard_rows % 8 == 0
+    dense_width = 4 * model_width + expert_count
+    full_width = -(-dense_width // lane_count) * lane_count
+    shard = jnp.concatenate(
+        [
+            attn_qkv,
+            attn_out,
+            router,
+            jnp.zeros((shard_rows, full_width - dense_width), jnp.bfloat16),
+        ],
+        axis=1,
+    )
+    if direct:
+        full = gather_rows(shard)
+    else:
+        full = lax.all_gather(shard, ("exp", "dp"), axis=0, tiled=True)
+    full_qkv = full[:, : 3 * model_width]
+    full_out = full[:, 3 * model_width : 4 * model_width]
+    full_route = full[:, 4 * model_width : dense_width]
     inputs = hidden_in.astype(jnp.float32)
     normed, attn_norm_pull = jax.vjp(rms_norm, inputs, gain_attn)
     normed_low = normed.astype(jnp.bfloat16)
@@ -83,7 +356,15 @@
     key_rows = qkv_low[:, model_width : 2 * model_width].reshape(row_count, head_count, head_size)
     value_rows = qkv_low[:, 2 * model_width :].reshape(row_count, head_count, head_size)
     bucket_ids = bucket_table(row_count, bucket_count)
-    pos_bias = jnp.transpose(jnp.take(rel_bias, bucket_ids, axis=0), (2, 0, 1))
+    bucket_hot = jnp.asarray(
+        bucket_ids.reshape(1, -1) == np.arange(bucket_count)[:, None], dtype=jnp.bfloat16
+    )
+    pos_bias = jnp.einsum(
+        "bh,bn->hn",
+        rel_bias,
+        bucket_hot.astype(jnp.float32),
+        precision=lax.Precision.HIGHEST,
+    ).reshape(head_count, row_count, row_count)
     segment = segment_ids(lengths, row_count)[0]
     allowed = (segment[:, None] == segment[None, :])[None]
     scores = score_block(queries, key_rows, pos_bias, allowed, score_scale)
@@ -111,65 +392,58 @@
     dispatch = (
         jnp.arange(expert_count * capacity, dtype=jnp.int32)[:, None] == slot_place[None, :]
     ).astype(jnp.bfloat16)
-    outgoing = jnp.dot(dispatch, ffn_low, preferred_element_type=jnp.float32).astype(jnp.bfloat16)
-    outgoing = outgoing.reshape(group_count, local_count, capacity, model_width)
+    grad_out = cotangent.astype(jnp.float32)
+    grad_picked = (gate_prob * grad_out).astype(jnp.bfloat16)
+    outgoing = jnp.dot(
+        dispatch,
+        jnp.concatenate([ffn_low, grad_picked], axis=1),
+        preferred_element_type=jnp.float32,
+    ).astype(jnp.bfloat16)
+    outgoing = outgoing.reshape(group_count, local_count, capacity, 2 * model_width)
     arrived = lax.all_to_all(outgoing, "exp", split_axis=0, concat_axis=0, tiled=True)
-    expert_rows = lax.all_gather(arrived[None], "dp", axis=0, tiled=True)
+    gathered = lax.all_gather(arrived[None], "dp", axis=0, tiled=True)
+    slot_rows = dp_count * group_count * capacity
+    gathered = jnp.transpose(gathered, (2, 0, 1, 3, 4)).reshape(
+        local_count, slot_rows, 2 * model_width
+    )
+    expert_rows = gathered[:, :, :model_width]
+    grad_result = gathered[:, :, model_width:]
     hidden_pre = jnp.einsum(
-        "rslcd,ldf->rslcf", expert_rows, expert_in, preferred_element_type=jnp.float32
+        "lsd,ldf->lsf", expert_rows, expert_in, preferred_element_type=jnp.float32
     )
     active_f32, gelu_pull = jax.vjp(gelu_tanh, hidden_pre)
     active = active_f32.astype(jnp.bfloat16)
-    partial_out = jnp.einsum(
-        "rslcf,lfd->rslcd", active, expert_out, preferred_element_type=jnp.float32
-    )
-    result_rows = (
-        lax.psum_scatter(partial_out.astype(jnp.bfloat16), "dp", scatter_dimension=0, tiled=True)
-        .astype(jnp.float32)[0]
-        .astype(jnp.bfloat16)
-    )
+    partial_out = jnp.einsum("lsf,lfd->lsd", active, expert_out, preferred_element_type=jnp.float32)
+    grad_active = jnp.einsum(
+        "lsd,lfd->lsf", grad_result, expert_out, preferred_element_type=jnp.float32
+    )
+    grad_pre = gelu_pull(grad_active)[0].astype(jnp.bfloat16)
+    grad_part = jnp.einsum("lsf,ldf->lsd", grad_pre, expert_in, preferred_element_type=jnp.float32)
+    grad_expert_out = jnp.einsum(
+        "lsf,lsd->lfd", active, grad_result, preferred_element_type=jnp.float32
+    )
+    grad_expert_in = jnp.einsum(
+        "lsd,lsf->ldf", expert_rows, grad_pre, preferred_element_type=jnp.float32
+    )
+    partial = jnp.concatenate(
+        [partial_out.astype(jnp.bfloat16), grad_part.astype(jnp.bfloat16)], axis=2
+    ).reshape(local_count, dp_count, group_count, capacity, 2 * model_width)
+    partial = jnp.transpose(partial, (1, 2, 0, 3, 4))
+    result_rows = lax.psum_scatter(partial, "dp", scatter_dimension=0, tiled=True)[0]
     returned = lax.all_to_all(result_rows, "exp", split_axis=0, concat_axis=0, tiled=True)
-    picked = jnp.take(
-        returned.reshape(expert_count * capacity, model_width), slot_place, axis=0
-    ).astype(jnp.float32)
+    picked_both = lax.dot_general(
+        dispatch,
+        returned.reshape(expert_count * capacity, 2 * model_width),
+        (((0,), (0,)), ((), ())),
+        preferred_element_type=jnp.float32,
+    )
+    picked = picked_both[:, :model_width]
+    grad_ffn = picked_both[:, model_width:]
     mixed = (middle + gate_prob * picked).astype(jnp.bfloat16)
-    full_qkv, full_out, full_route = (
-        lax.all_gather(attn_qkv, ("exp", "dp"), axis=0, tiled=True),
-        lax.all_gather(attn_out, ("exp", "dp"), axis=0, tiled=True),
-        lax.all_gather(router, ("exp", "dp"), axis=0, tiled=True),
-    )
-    grad_out = cotangent.astype(jnp.float32)
-    grad_picked = (gate_prob * grad_out).astype(jnp.bfloat16)
     gate_grad = jnp.sum(grad_out * picked, axis=1, keepdims=True)
     logit_grad = (gate_probs * (jnp.where(choose, gate_grad, 0.0) - gate_prob * gate_grad)).astype(
         jnp.bfloat16
     )
-    grad_slots = jnp.dot(dispatch, grad_picked, preferred_element_type=jnp.float32).astype(
-        jnp.bfloat16
-    )
-    grad_slots = grad_slots.reshape(group_count, local_count, capacity, model_width)
-    grad_arrived = lax.all_to_all(grad_slots, "exp", split_axis=0, concat_axis=0, tiled=True)
-    grad_result = lax.all_gather(grad_arrived[None], "dp", axis=0, tiled=True)
-    grad_active = jnp.einsum(
-        "rslcd,lfd->rslcf", grad_result, expert_out, preferred_element_type=jnp.float32
-    )
-    grad_pre = gelu_pull(grad_active)[0].astype(jnp.bfloat16)
-    grad_expert_out = jnp.einsum(
-        "rslcf,rslcd->lfd", active, grad_result, preferred_element_type=jnp.float32
-    )
-    grad_expert_in = jnp.einsum(
-        "rslcd,rslcf->ldf", expert_rows, grad_pre, preferred_element_type=jnp.float32
-    )
-    grad_part = jnp.einsum(
-        "rslcf,ldf->rslcd", grad_pre, expert_in, preferred_element_type=jnp.float32
-    )
-    grad_rows = lax.psum_scatter(
-        grad_part.astype(jnp.bfloat16), "dp", scatter_dimension=0, tiled=True
-    ).astype(jnp.float32)[0]
-    grad_back = lax.all_to_all(
-        grad_rows.astype(jnp.bfloat16), "exp", split_axis=0, concat_axis=0, tiled=True
-    ).astype(grad_rows.dtype)
-    grad_ffn = jnp.take(grad_back.reshape(expert_count * capacity, model_width), slot_place, axis=0)
     grad_ffn = grad_ffn + jnp.dot(logit_grad, full_route.T, preferred_element_type=jnp.float32)
     grad_router = jnp.einsum("td,te->de", ffn_low, logit_grad, preferred_element_type=jnp.float32)
     grad_middle_norm, grad_gain_ffn = ffn_norm_pull(grad_ffn)
@@ -203,11 +477,8 @@
         jnp.einsum("hqk,qhe->khe", grad_scores, queries, preferred_element_type=jnp.float32)
         * score_scale
     )
-    bucket_hot = jnp.asarray(
-        bucket_ids.reshape(-1)[:, None] == np.arange(bucket_count)[None, :], dtype=jnp.bfloat16
-    )
     grad_bias = jnp.einsum(
-        "nb,hn->bh",
+        "bn,hn->bh",
         bucket_hot,
         grad_scores.reshape(head_count, row_count * row_count),
         preferred_element_type=jnp.float32,
@@ -226,28 +497,46 @@
     grad_normed = jnp.dot(grad_qkv, full_qkv.T, preferred_element_type=jnp.float32)
     grad_inputs_norm, grad_gain_attn = attn_norm_pull(grad_normed)
     grad_in = grad_middle + grad_inputs_norm
-    stacked = jnp.concatenate([grad_attn_qkv, grad_attn_out, grad_router], axis=1)
-    total_width = stacked.shape[1]
-    dp_count = lax.axis_size("dp")
-    shard_rows = model_width // (group_count * dp_count)
-    pieces = lax.all_to_all(
-        stacked.reshape(group_count, dp_count * shard_rows, total_width).astype(jnp.bfloat16),
-        "exp",
-        split_axis=0,
-        concat_axis=0,
-        tiled=True,
-    ).astype(jnp.float32)
-    partial_value = jnp.sum(pieces, axis=0).reshape(dp_count, shard_rows, total_width)
-    pieces = lax.all_to_all(
-        partial_value.astype(jnp.bfloat16), "dp", split_axis=0, concat_axis=0, tiled=True
-    ).astype(partial_value.dtype)
-    owned = jnp.sum(pieces, axis=0)
+    stacked = jnp.concatenate(
+        [
+            grad_attn_qkv.astype(jnp.bfloat16),
+            grad_attn_out.astype(jnp.bfloat16),
+            grad_router.astype(jnp.bfloat16),
+            jnp.zeros((model_width, full_width - dense_width), jnp.bfloat16),
+        ],
+        axis=1,
+    )
+    if direct:
+        small = jnp.concatenate([grad_gain_attn, grad_gain_ffn, grad_bias.reshape(-1)])
+        small_size = small.shape[0]
+        small_rows = -(-small_size // (8 * lane_count)) * 8
+        small = jnp.pad(small, (0, small_rows * lane_count - small_size))
+        owned, small = reduce_rows(
+            stacked.reshape(-1, shard_rows, full_width), small.reshape(small_rows, lane_count)
+        )
+        small = small.reshape(-1)
+        grad_gain_attn = small[:model_width]
+        grad_gain_ffn = small[model_width : 2 * model_width]
+        grad_bias = small[2 * model_width : small_size].reshape(bucket_count, head_count)
+    else:
+        pieces = lax.all_to_all(
+            stacked.reshape(group_count, dp_count * shard_rows, full_width),
+            "exp",
+            split_axis=0,
+            concat_axis=0,
+            tiled=True,
+        ).astype(jnp.float32)
+        pieces = jnp.sum(pieces, axis=0).reshape(dp_count, shard_rows, full_width)
+        pieces = lax.all_to_all(
+            pieces.astype(jnp.bfloat16), "dp", split_axis=0, concat_axis=0, tiled=True
+        ).astype(jnp.float32)
+        owned = jnp.sum(pieces, axis=0)
+        grad_gain_attn, grad_gain_ffn, grad_bias = lax.psum(
+            (grad_gain_attn, grad_gain_ffn, grad_bias), ("exp", "dp")
+        )
     grad_attn_qkv = owned[:, : 3 * model_width]
     grad_attn_out = owned[:, 3 * model_width : 4 * model_width]
-    grad_router = owned[:, 4 * model_width :]
-    grad_gain_attn, grad_gain_ffn, grad_bias = lax.psum(
-        (grad_gain_attn, grad_gain_ffn, grad_bias), ("exp", "dp")
-    )
+    grad_router = owned[:, 4 * model_width : dense_width]
     return (
         mixed,
         grad_in,

time: 421 us -> 299 us (0.71)
  blocking collectives: 163 us -> 12.8 us
  Pallas kernels: 0 us -> 78.6 us
  local copies, waits for them, and re-layouts: 87.9 us -> 47.8 us
  starting transfers between devices: 20.9 us -> 4.62 us
  matrix products: 38.2 us -> 45 us
  other arithmetic: 17.2 us -> 10.8 us
  waiting for transfers between devices: 78 us -> 83.5 us
    all_gather x3 -> x0, blocking collectives: 113 us -> none  [the longest x1 70.9 us: local(): lax.all_gather(router, ('exp', 'dp'), axis=0, tiled=True)]
    pallas_call x0 -> x2, Pallas kernels: none -> 78.6 us  [the longest x1 45.5 us: reduce_rows(): pl.pallas_call(reduce_kernel, out_shape=(jax.ShapeDtypeStruct((rows, widt...]
    gather x4 -> x0, local copies, waits for them, and re-layouts: 65 us -> none  [the longest x2 62.3 us: local(): pos_bias = jnp.transpose(jnp.take(rel_bias, bucket_ids, axis=0), (2, 0, 1))]
    all_to_all x4 -> x0, waiting for transfers between devices: 57.3 us -> none  [the longest x1 47.1 us: local(): lax.all_to_all(stacked.reshape(group_count, dp_count * shard_rows, total_...]
    all_gather x2 -> x1, waiting for transfers between devices: 0.04 us -> 42.9 us  [local(): gathered = lax.all_gather(arrived[None], 'dp', axis=0, tiled=True)]
    psum x1 -> x0, blocking collectives: 40 us -> none  [local(): lax.psum((grad_gain_attn, grad_gain_ffn, grad_bias), ('exp', 'dp'))]
    reduce_scatter x2 -> x1, waiting for transfers between devices: 19.2 us -> 40.4 us  [local(): lax.psum_scatter(partial, 'dp', scatter_dimension=0, tiled=True)[0]]
    all_to_all x4 -> x0, starting transfers between devices: 17.1 us -> none  [the longest x1 5 us: local(): lax.all_to_all(stacked.reshape(group_count, dp_count * shard_rows, total_...]
  transfers between devices with their start and end apart: 9 -> 3, of which waited for: 4 -> 3; matrix products, arithmetic and copies ran while one was open for 26% -> 3% of each run, Pallas kernels for 0% -> 0%
where the time goes in v1:
time: 299 us; the launch traced here: 298 us
  waiting for transfers between devices  83.5 us (28%)
  Pallas kernels  78.6 us (26%)
  local copies, waits for them, and re-layouts  47.8 us (16%)
  matrix products  45 us (15%)
  between operations  14.9 us (5%)
  blocking collectives  12.8 us (4%)
  other arithmetic  10.8 us (4%)
  starting transfers between devices  4.62 us (2%)
    pallas_call x1, Pallas kernels, reduce_rows(): pl.pallas_call(reduce_kernel, out_shape=(jax.ShapeDtypeStruct((rows, widt...  45.5 us
    all_gather x1, waiting for transfers between devices, local(): gathered = lax.all_gather(arrived[None], 'dp', axis=0, tiled=True)  42.9 us
    reduce_scatter x1, waiting for transfers between devices, local(): lax.psum_scatter(partial, 'dp', scatter_dimension=0, tiled=True)[0]  40.4 us
    pallas_call x1, Pallas kernels, gather_rows(): pl.pallas_call(gather_kernel, out_shape=jax.ShapeDtypeStruct((32, rows, w...  33.2 us
    all_to_all x1, blocking collectives, local(): lax.all_to_all(outgoing, 'exp', split_axis=0, concat_axis=0, tiled=True)  12.8 us
    unnamed x120, local copies, waits for them, and re-layouts  10.9 us
    concatenate x1, local copies, waits for them, and re-layouts, local(): jnp.concatenate([grad_attn_qkv.astype(jnp.bfloat16), grad_attn_out.astype...  7.89 us
  transfers between devices with their start and end apart: 3, of which 3 were waited for; matrix products, arithmetic and copies ran while one was open for 3% of the time, Pallas kernels for 0%

profile of v1, /device:TPU:0, one launch (start us, length us, event | category | flops | bytes accessed | tf_op | source)
XLA Modules:
  0.0 297.9 jit_solution(7208457310446996130)
XLA Ops:
  7.2 0.9 copy.164
  8.2 1.6 concatenate.19.mine_ref
  9.8 33.2 %gather_rows.1 = bf16[32,24,3200]{2,1,0:T(8,128)(2,1)} custom-call(bf16[24,3200]{1,0:T(8,128)(2,1)} %concatenate.19.mine_ref), custom_call_target="tpu_custom_call" | custom-call | bytes 4915200 | tf_op jit(solution)/shard_map/gather_rows/pallas_call | solution.py:153
  43.7 2.7 convolution_convert_fusion.1
  46.4 0.7 fusion.62
  47.5 1.9 fusion.65
  49.6 1.1 copy.168
  51.1 1.5 fusion.63
  52.8 1.1 copy.165
  54.6 1.8 multiply_reduce_fusion.3
  57.0 0.7 copy-done.13
  57.7 1.1 fusion.64
  58.9 0.6 fusion.52
  60.1 0.5 select_reduce_fusion.1
  60.6 1.4 copy.170
  62.0 1.6 reduce_window_sum.23
  63.6 1.5 copy.171
  65.2 0.7 select_reduce_fusion
  65.9 0.7 multiply_add_fusion
  66.5 1.0 fusion.31
  67.6 2.0 convolution_convert_fusion.2
  69.6 2.1 reshape.232
  71.6 1.6 copy.172
  73.3 12.8 %all_to_all.10 = bf16[8,2,10,1536]{3,1,2,0:T(2,128)(2,1)} all-to-all(bf16[8,2,10,1536]{3,1,2,0:T(2,128)(2,1)S(1)} %copy.172), channel_id=1, replica_groups=mesh['exp'=8,'dp'=4] {'exp'}, dimensions={0} | all-to-all | bytes 983040 | tf_op jit(solution)/shard_map/all_to_all | solution.py:403
  86.3 42.9 %all-gather.3.cloned.1.call-done = bf16[32,2,10,1536]{3,1,2,0:T(2,128)(2,1)} async-done(((bf16[8,2,10,1536]{3,1,2,0:T(2,128)(2,1)}), bf16[32,2,10,1536]{3,1,2,0:T(2,128)(2,1)}) %all-gather.3.cloned.1.call-update) | async-done | bytes 1966096 | tf_op jit(solution)/shard_map/all_gather | solution.py:404
  129.2 2.7 fusion.61
  132.0 1.0 copy-done.2
  132.9 0.9 fusion.24
  133.9 1.1 convolution_convert_fusion.5
  135.2 1.9 fusion.9
  137.1 1.0 convolution_convert_fusion.4
  138.2 2.0 copy.175
  140.3 1.6 copy.176
  141.9 40.4 %reduce-scatter.2.cloned.1.call-done = bf16[1,8,2,10,1536]{4,1,3,2,0:T(8,128)(2,1)} async-done(((bf16[4,8,2,10,1536]{4,1,3,2,0:T(8,128)(2,1)}), bf16[1,8,2,10,1536]{4,1,3,2,0:T(8,128)(2,1)}) %reduce-scatter.2.cloned.1.call-update) | async-done | bytes 491536 | tf_op jit(solution)/shard_map/reduce_scatter | solution.py:432
  182.3 2.3 copy.177
  184.7 4.4 %all-to-all-start.1 = ((bf16[8,2,10,1536]{3,1,2,0:T(2,128)(2,1)}), bf16[8,2,10,1536]{3,1,2,0:T(2,128)(2,1)}, u32[]{:S(2)}, u32[]{:S(2)}) async-start(bf16[8,2,10,1536]{3,1,2,0:T(2,128)(2,1)} %copy.177), calls=%async_computation.2 | async-start | bytes 983040 | tf_op jit(solution)/shard_map/all_to_all | solution.py:433
  189.0 5.3 %fusion.22 = f32[2,768,768]{2,1,0:T(8,128)} fusion(bf16[2,320,768]{2,1,0:T(8,128)(2,1)} %copy-done.24, bf16[2,320,768]{2,0,1:T(2,128)(2,1)} %copy-done.2), kind=kOutput, calls=%fused_computation.39 | convolution fusion | flops 754974720 | bytes 6684672 | tf_op jit(solution)/shard_map/lsd,lsf->ldf/dot_general | solution.py:425
  194.3 3.8 %fusion.16 = f32[2,768,768]{2,1,0:T(8,128)} fusion(bf16[2,320,768]{2,0,1:T(2,128)(2,1)S(1)} %copy-done.12, f32[2,320,768]{2,1,0:T(8,128)S(1)} %copy-done.4), kind=kOutput, calls=%fused_computation.35 | convolution fusion | flops 759398400 | bytes 7667712 | tf_op jit(solution)/shard_map/lsf,lsd->lfd/dot_general | solution.py:422
  198.2 2.0 copy.178
  200.3 2.1 reshape.235
  202.4 1.4 fusion.46
  203.9 1.7 fusion.32
  205.7 1.9 multiply_reduce_fusion.1
  207.8 0.7 copy-done.5
  208.5 1.8 convolution_convert_fusion.7
  210.5 1.3 multiply_reduce_fusion
  211.8 0.9 multiply_convert_fusion.1
  212.8 2.0 copy.185
  214.8 1.4 fusion.12
  216.2 1.5 fusion.13
  217.7 1.3 convolution_convert_fusion.6
  219.3 1.6 convolution_convert_fusion.3
  220.9 4.1 %fusion.30 = (f32[768]{0:T(1024)S(1)}, f32[128]{0:T(128)S(1)}, f32[128,768]{1,0:T(8,128)}) fusion(bf16[128,768]{1,0:T(8,128)(2,1)S(1)} %copy-done.8, f32[128]{0:T(128)S(1)} %copy-done.42, f32[768]{0:T(1024)S(1)} %copy-done.26, bf16[768,3200]{1,0:T(8,128)(2,1)} %bitcast.74, bf16[128,768]{0,1:T(8,128)(2,1)S(1)} %bitcast.91, ...), kind=kOutput, calls=%fused_computation.61 | convolution fusion | flops 455441536 | bytes 4725760 | tf_op jit(solution)/shard_map/dot_general | solution.py:497
  224.9 3.0 %convolution_convert_fusion = bf16[768,2304]{1,0:T(8,128)(2,1)} fusion(bf16[128,768]{0,1:T(8,128)(2,1)S(1)} %bitcast.92, bf16[128,768]{0,1:T(8,128)(2,1)S(1)} %bitcast.96, bf16[128,768]{0,1:T(8,128)(2,1)S(1)} %bitcast.94, bf16[128,768]{1,0:T(8,128)(2,1)S(1)} %copy-done.8, f32[768]{0:T(1024)S(1)} %copy-done.26, f32[128]{0:T(128)S(1)} %copy-done.42), kind=kOutput, calls=%fused_computation | convolution fusion | flops 456916992 | bytes 4328960 | tf_op jit(solution)/shard_map/td,tf->df/dot_general | solution.py:494
  228.4 0.8 copy-done.10
  230.0 7.9 %concatenate.23 = bf16[768,3200]{1,0:T(8,128)(2,1)} concatenate(bf16[768,2304]{1,0:T(8,128)(2,1)} %convolution_convert_fusion, bf16[768,768]{1,0:T(8,128)(2,1)} %convolution_convert_fusion.3, bf16[768,16]{1,0:T(8,128)(2,1)S(1)} %copy.184, bf16[768,112]{1,0:T(8,128)(2,1)S(1)} %broadcast_in_dim.74), dimensions={1} | concatenate | bytes 9830400 | tf_op jit(solution)/shard_map/concatenate | solution.py:500
  237.9 2.4 copy-done.1
  240.3 45.5 %reduce_rows.1 = (f32[24,3200]{1,0:T(8,128)S(1)}, f32[16,128]{1,0:T(8,128)S(1)}) custom-call(bf16[32,24,3200]{2,1,0:T(8,128)(2,1)S(1)} %bitcast.68, f32[16,128]{1,0:T(8,128)S(1)} %fusion.51.small_ref), custom_call_target="tpu_custom_call" | custom-call | flops 4915200 | bytes 4915200 | tf_op jit(solution)/shard_map/reduce_rows/pallas_call | solution.py:275
  285.8 0.7 slice.67
  286.5 0.6 slice.68
  287.1 0.6 slice_bitcast_fusion
  287.8 0.7 copy.187
  288.5 0.7 copy.188
  289.2 1.9 fusion.33
  (147 shorter events, 6.3 us)
Async XLA Ops:
  7.2 126.7 %copy-start = (bf16[2,768,768]{2,1,0:T(8,128)(2,1)S(1)}, bf16[2,768,768]{2,1,0:T(8,128)(2,1)}, u32[]{:S(2)}) copy-start(bf16[2,768,768]{2,1,0:T(8,128)(2,1)} %param.24) | copy-start | bytes 7077892
  7.2 122.0 %all-gather.3.cloned.1.call-start = ((), (), s32[]{:S(2)}) async-start(), calls=%async_computation.4 | async-start | bytes 2457600 | tf_op jit(solution)/shard_map/all_gather | solution.py:404
  9.8 33.2 %copy-start.7 = (bf16[128,768]{1,0:T(8,128)(2,1)S(1)}, bf16[128,768]{1,0:T(8,128)(2,1)}, u32[]{:S(2)}) copy-start(bf16[128,768]{1,0:T(8,128)(2,1)} %param.13) | copy-start | bytes 589828
  9.8 33.9 %copy-start.25 = (f32[768]{0:T(1024)S(1)}, f32[768]{0:T(1024)}, u32[]{:S(2)}) copy-start(f32[768]{0:T(1024)} %param.17) | copy-start | bytes 9220
  43.1 0.5 copy-start.52
  43.1 0.6 copy-start.41
  46.4 1.1 copy-start.37
  47.3 3.9 %copy-start.21 = (bf16[128,768]{0,1:T(8,128)(2,1)}, bf16[128,768]{0,1:T(8,128)(2,1)S(1)}, u32[]{:S(2)}) copy-start(bf16[128,768]{0,1:T(8,128)(2,1)S(1)} %copy.166) | copy-start | bytes 589828
  47.5 3.7 %copy-start.22 = (bf16[128,768]{0,1:T(8,128)(2,1)}, bf16[128,768]{0,1:T(8,128)(2,1)S(1)}, u32[]{:S(2)}) copy-start(bf16[128,768]{0,1:T(8,128)(2,1)S(1)} %copy.167) | copy-start | bytes 589828
  49.5 1.2 copy-start.56
  52.8 4.2 %copy-start.28 = (f32[768]{0:T(1024)S(1)}, f32[768]{0:T(1024)}, u32[]{:S(2)}) copy-start(f32[768]{0:T(1024)} %param.21) | copy-start | bytes 9220
  53.9 0.7 copy-start.19
  53.9 5.0 %copy-start.34 = (s32[128,1]{0,1:T(1,128)S(1)}, s32[128,1]{0,1:T(1,128)}, u32[]{:S(2)}) copy-start(s32[128,1]{0,1:T(1,128)} %param.16) | copy-start | bytes 1540
  54.6 4.3 %copy-start.16 = (bf16[12,64,128]{2,1,0:T(8,128)(2,1)}, bf16[12,64,128]{2,1,0:T(8,128)(2,1)S(1)}, u32[]{:S(2)}) copy-start(bf16[12,64,128]{2,1,0:T(8,128)(2,1)S(1)} %convolution_convert_fusion.8) | copy-start | bytes 589828
  56.4 3.1 %copy-start.54 = (f32[128]{0:T(128)}, f32[128]{0:T(128)S(1)}, u32[]{:S(2)}) copy-start(f32[128]{0:T(128)S(1)} %get-tuple-element.99) | copy-start | bytes 1540
  56.4 0.5 copy-start.47
  57.0 0.7 copy-start.13
  58.9 0.7 copy-start.31
  59.5 0.5 copy-start.38
  66.5 1.0 copy-start.49
  86.1 96.3 %reduce-scatter.2.cloned.1.call-start = ((), (), s32[]{:S(2)}) async-start(), calls=%async_computation.3 | async-start | bytes 2457600 | tf_op jit(solution)/shard_map/reduce_scatter | solution.py:432
  129.2 3.7 %copy-start.15 = (bf16[2,768,768]{2,1,0:T(8,128)(2,1)S(1)}, bf16[2,768,768]{2,1,0:T(8,128)(2,1)}, u32[]{:S(2)}) copy-start(bf16[2,768,768]{2,1,0:T(8,128)(2,1)} %param.23) | copy-start | bytes 7077892
  131.9 1.0 copy-start.2
  131.9 3.0 %copy-start.11 = (bf16[2,320,768]{2,0,1:T(2,128)(2,1)}, bf16[2,320,768]{2,0,1:T(2,128)(2,1)S(1)}, u32[]{:S(2)}) copy-start(bf16[2,320,768]{2,0,1:T(2,128)(2,1)S(1)} %get-tuple-element.88) | copy-start | bytes 2949124
  133.9 1.3 copy-start.3
  137.1 1.0 copy-start.24
  184.7 13.6 %all-to-all-start.1 = ((bf16[8,2,10,1536]{3,1,2,0:T(2,128)(2,1)}), bf16[8,2,10,1536]{3,1,2,0:T(2,128)(2,1)}, u32[]{:S(2)}, u32[]{:S(2)}) async-start(bf16[8,2,10,1536]{3,1,2,0:T(2,128)(2,1)} %copy.177), calls=%async_computation.2 | async-start | bytes 983040 | tf_op jit(solution)/shard_map/all_to_all | solution.py:433
  189.0 5.3 %copy-start.4 = (f32[2,320,768]{2,1,0:T(8,128)S(1)}, f32[2,320,768]{2,1,0:T(8,128)}, u32[]{:S(2)}) copy-start(f32[2,320,768]{2,1,0:T(8,128)} %copy-done.3) | copy-start | bytes 5898244
  189.0 5.3 %copy-start.12 = (bf16[2,320,768]{2,0,1:T(2,128)(2,1)S(1)}, bf16[2,320,768]{2,0,1:T(2,128)(2,1)}, u32[]{:S(2)}) copy-start(bf16[2,320,768]{2,0,1:T(2,128)(2,1)} %copy-done.11) | copy-start | bytes 2949124
  202.4 3.2 %copy-start.46 = (f32[128]{0:T(128)S(1)}, f32[128]{0:T(128)}, u32[]{:S(2)}) copy-start(f32[128]{0:T(128)} %select_reduce_fusion.1) | copy-start | bytes 1540
  202.4 3.2 %copy-start.29 = (f32[768]{0:T(1024)S(1)}, f32[768]{0:T(1024)}, u32[]{:S(2)}) copy-start(f32[768]{0:T(1024)} %param.21) | copy-start | bytes 9220
  202.4 3.2 %copy-start.32 = (f32[128]{0:T(128)S(1)}, f32[128]{0:T(128)}, u32[]{:S(2)}) copy-start(f32[128]{0:T(128)} %copy-done.31) | copy-start | bytes 1540
  202.4 3.2 %copy-start.35 = (s32[128,1]{0,1:T(1,128)S(1)}, s32[128,1]{0,1:T(1,128)}, u32[]{:S(2)}) copy-start(s32[128,1]{0,1:T(1,128)} %param.16) | copy-start | bytes 1540
  202.4 3.2 %copy-start.39 = (f32[128]{0:T(128)S(1)}, f32[128]{0:T(128)}, u32[]{:S(2)}) copy-start(f32[128]{0:T(128)} %copy-done.38) | copy-start | bytes 1540
  202.4 3.2 %copy-start.48 = (f32[128]{0:T(128)S(1)}, f32[128]{0:T(128)}, u32[]{:S(2)}) copy-start(f32[128]{0:T(128)} %copy-done.47) | copy-start | bytes 1540
  202.4 5.1 %copy-start.55 = (f32[128]{0:T(128)S(1)}, f32[128]{0:T(128)}, u32[]{:S(2)}) copy-start(f32[128]{0:T(128)} %copy-done.54) | copy-start | bytes 1540
  202.4 5.2 %copy-start.18 = (bf16[128,768]{1,0:T(8,128)(2,1)S(1)}, bf16[128,768]{1,0:T(8,128)(2,1)}, u32[]{:S(2)}) copy-start(bf16[128,768]{1,0:T(8,128)(2,1)} %param.14) | copy-start | bytes 589828
  205.6 2.0 copy-start.44
  205.6 1.9 copy-start.50
  207.7 0.7 copy-start.5
  210.5 1.3 copy-start.20
  212.8 6.5 %copy-start.6 = (f32[128,768]{1,0:T(8,128)S(1)}, f32[128,768]{1,0:T(8,128)}, u32[]{:S(2)}) copy-start(f32[128,768]{1,0:T(8,128)} %copy-done.5) | copy-start | bytes 1179652
  214.7 4.3 %copy-start.14 = (bf16[128,768]{1,0:T(8,128)(2,1)S(1)}, bf16[128,768]{1,0:T(8,128)(2,1)}, u32[]{:S(2)}) copy-start(bf16[128,768]{1,0:T(8,128)(2,1)} %copy-done.13) | copy-start | bytes 589828
  214.7 4.3 %copy-start.33 = (f32[128]{0:T(128)S(1)}, f32[128]{0:T(128)}, u32[]{:S(2)}) copy-start(f32[128]{0:T(128)} %copy-done.31) | copy-start | bytes 1540
  214.7 4.4 %copy-start.36 = (s32[128,1]{0,1:T(1,128)S(1)}, s32[128,1]{0,1:T(1,128)}, u32[]{:S(2)}) copy-start(s32[128,1]{0,1:T(1,128)} %param.16) | copy-start | bytes 1540
  214.7 4.4 %copy-start.40 = (f32[128]{0:T(128)S(1)}, f32[128]{0:T(128)}, u32[]{:S(2)}) copy-start(f32[128]{0:T(128)} %copy-done.38) | copy-start | bytes 1540
  214.7 4.4 %copy-start.45 = (f32[128]{0:T(128)S(1)}, f32[128]{0:T(128)}, u32[]{:S(2)}) copy-start(f32[128]{0:T(128)} %copy-done.44) | copy-start | bytes 1540
  214.7 4.4 %copy-start.51 = (f32[128]{0:T(128)S(1)}, f32[128]{0:T(128)}, u32[]{:S(2)}) copy-start(f32[128]{0:T(128)} %copy-done.50) | copy-start | bytes 1540
  214.8 4.5 %copy-start.17 = (bf16[12,64,128]{2,1,0:T(8,128)(2,1)S(1)}, bf16[12,64,128]{2,1,0:T(8,128)(2,1)}, u32[]{:S(2)}) copy-start(bf16[12,64,128]{2,1,0:T(8,128)(2,1)} %copy-done.16) | copy-start | bytes 589828
  216.2 4.6 %copy-start.8 = (bf16[128,768]{1,0:T(8,128)(2,1)S(1)}, bf16[128,768]{1,0:T(8,128)(2,1)}, u32[]{:S(2)}) copy-start(bf16[128,768]{1,0:T(8,128)(2,1)} %param.13) | copy-start | bytes 589828
  216.2 4.6 %copy-start.26 = (f32[768]{0:T(1024)S(1)}, f32[768]{0:T(1024)}, u32[]{:S(2)}) copy-start(f32[768]{0:T(1024)} %param.17) | copy-start | bytes 9220
  216.2 4.6 %copy-start.42 = (f32[128]{0:T(128)S(1)}, f32[128]{0:T(128)}, u32[]{:S(2)}) copy-start(f32[128]{0:T(128)} %copy-done.41) | copy-start | bytes 1540
  224.9 3.0 %copy-start.23 = (bf16[12,128,128]{2,1,0:T(8,128)(2,1)S(1)}, bf16[12,128,128]{2,1,0:T(8,128)(2,1)}, u32[]{:S(2)}) copy-start(bf16[12,128,128]{2,1,0:T(8,128)(2,1)} %copy.185) | copy-start | bytes 1179652
  228.0 1.2 copy-start.10
  228.0 1.9 copy-start.30
  237.9 2.4 copy-start.1
  240.2 48.9 %copy-start.53 = (f32[128]{0:T(128)S(1)}, f32[128]{0:T(128)}, u32[]{:S(2)}) copy-start(f32[128]{0:T(128)} %copy-done.52) | copy-start | bytes 1540
  240.2 48.9 %copy-start.9 = (bf16[128,768]{1,0:T(8,128)(2,1)S(1)}, bf16[128,768]{1,0:T(8,128)(2,1)}, u32[]{:S(2)}) copy-start(bf16[128,768]{1,0:T(8,128)(2,1)} %param.13) | copy-start | bytes 589828
  240.3 48.9 %copy-start.27 = (f32[768]{0:T(1024)S(1)}, f32[768]{0:T(1024)}, u32[]{:S(2)}) copy-start(f32[768]{0:T(1024)} %param.17) | copy-start | bytes 9220
  240.3 48.9 %copy-start.43 = (f32[128]{0:T(128)S(1)}, f32[128]{0:T(128)}, u32[]{:S(2)}) copy-start(f32[128]{0:T(128)} %copy-done.41) | copy-start | bytes 1540
Sparse Core Ops, SparseCore 0:
  86.2 42.9 all-gather.2
  142.0 40.2 reduce-scatter.1

commit v2 on v1

--- a/solution.py
+++ b/solution.py
@@ -168,8 +168,9 @@
 
 
 def reduce_kernel(
-    grad_ref, small_ref, out_ref, total_ref,
-    from_core, summed, passing, from_x, from_y, from_z,
+    normed_ref, attended_ref, ffn_ref, qkv_ref, branch_ref, logit_ref, small_ref,
+    out_ref, total_ref,
+    grad_ref, from_core, summed, passing, from_x, from_y, from_z,
     small_sum, small_in, small_z, send_sem, recv_sem, small_send, small_recv,
 ):
     e, z, step_core, chips = positions()
@@ -225,33 +226,40 @@
         small_sum[number + 1] = small_sum[number] + small_in[number]
         return copy
 
-    small_sum[0] = small_ref[...]
-    for chip in (3, 1, 2, 0):
-        for j in (0, 1, 3, 2):
-            place = (chips[chip] + step_core) * 4 + zs[j]
-            send(grad_ref.at[place], from_core.at[chip * 4 + j], partner, chip * 4 + j)
-    small_copies = [step_sum(0, partner)]
-    for j in (0, 1, 3, 2):
+    def make(chip):
+        count = normed_ref.shape[0] // 4
+        group = lax.div(chips[chip], 2)
+        here = pl.ds(pl.multiple_of(group * count, count), count)
+        column = 0
+        for left, right in ((normed_ref, qkv_ref), (attended_ref, branch_ref), (ffn_ref, logit_ref)):
+            width = right.shape[1]
+            step = width if width <= 768 else 768
+            for start in range(0, width, step):
+                part = jnp.dot(
+                    left[here, :], right[:, start : start + step],
+                    preferred_element_type=jnp.float32,
+                )
+                part = part.reshape(8, count // 8, step).astype(jnp.bfloat16)
+                grad_ref[pl.ds(group * 8, 8), :, column + start : column + start + step] = part
+            column += width
+
+    def diagonal(j):
         number = 12 + j
         summed[number] = pair(3, j).astype(jnp.bfloat16)
         device = beside[2] if j in by_y else beside[1]
         send(summed.at[number], passing.at[j], device, 16 + j)
-    small_copies.append(step_sum(1, beside[1]))
-    for j, chip in ((1, 1), (0, 2), (2, 1), (3, 2), (0, 1), (1, 2), (3, 1), (2, 2)):
-        number = chip * 4 + j
-        value = pair(chip, j)
-        if (j in by_y) == (chip == 1):
-            value = value + arrive(passing.at[j], 16 + j)
-        summed[number] = value.astype(jnp.bfloat16)
-        landing = from_x if chip == 1 else from_y
-        send(summed.at[number], landing.at[j], beside[chip], 16 + number)
-    small_copies.append(step_sum(2, beside[2]))
-    small_z[0] = small_sum[3]
-    for j in (1, 2, 3):
-        copy = small_copy(small_z.at[0], small_z.at[4 - j], along[j], 2 + j, 6 - j)
-        copy.start()
-        small_copies.append(copy)
-    for j in (1, 2, 3, 0):
+
+    def beside_chips(j):
+        for chip in (2, 1) if j in by_y else (1, 2):
+            number = chip * 4 + j
+            value = pair(chip, j)
+            if (j in by_y) == (chip == 1):
+                value = value + arrive(passing.at[j], 16 + j)
+            summed[number] = value.astype(jnp.bfloat16)
+            landing = from_x if chip == 1 else from_y
+            send(summed.at[number], landing.at[j], beside[chip], 16 + number)
+
+    def own_chip(j):
         value = pair(0, j) + arrive(from_x.at[j], 20 + j) + arrive(from_y.at[j], 24 + j)
         if j == 0:
             for other in (1, 2, 3):
@@ -260,6 +268,38 @@
         else:
             summed[j] = value.astype(jnp.bfloat16)
             send(summed.at[j], from_z.at[3 - j], along[j], 31 - j)
+
+    order = (2, 1, 3, 0)
+    small_sum[0] = small_ref[...]
+    for chip in (3, 1, 2, 0):
+        make(chip)
+        for j in order[:2]:
+            place = (chips[chip] + step_core) * 4 + zs[j]
+            send(grad_ref.at[place], from_core.at[chip * 4 + j], partner, chip * 4 + j)
+    for j in order[2:]:
+        for chip in (3, 1, 2, 0):
+            place = (chips[chip] + step_core) * 4 + zs[j]
+            send(grad_ref.at[place], from_core.at[chip * 4 + j], partner, chip * 4 + j)
+    diagonal(order[0])
+    diagonal(order[1])
+    beside_chips(order[0])
+    small_copies = [step_sum(0, partner)]
+    diagonal(order[2])
+    beside_chips(order[1])
+    own_chip(order[0])
+    small_copies.append(step_sum(1, beside[1]))
+    diagonal(order[3])
+    beside_chips(order[2])
+    own_chip(order[1])
+    small_copies.append(step_sum(2, beside[2]))
+    beside_chips(order[3])
+    small_z[0] = small_sum[3]
+    for j in (1, 2, 3):
+        copy = small_copy(small_z.at[0], small_z.at[4 - j], along[j], 2 + j, 6 - j)
+        copy.start()
+        small_copies.append(copy)
+    own_chip(order[2])
+    own_chip(order[3])
     for copy in small_copies[3:]:
         copy.wait_recv()
     spot = [lax.rem(4 + k - z, 4) for k in range(4)]
@@ -268,8 +308,8 @@
         copy.wait_send()
 
 
-def reduce_rows(grads, small):
-    _, rows, width = grads.shape
+def reduce_rows(operands, rows, small):
+    width = sum(right.shape[1] for right in operands[3:])
     vmem = pl.BlockSpec(memory_space=pltpu.VMEM)
     block = functools.partial(pltpu.VMEM, dtype=jnp.bfloat16)
     return pl.pallas_call(
@@ -278,9 +318,10 @@
             jax.ShapeDtypeStruct((rows, width), jnp.float32),
             jax.ShapeDtypeStruct(small.shape, jnp.float32),
         ),
-        in_specs=[vmem, vmem],
+        in_specs=[vmem] * 7,
         out_specs=(vmem, vmem),
         scratch_shapes=[
+            block((32, rows, width)),
             block((16, rows, width)),
             block((16, rows, width)),
             block((4, rows, width)),
@@ -299,10 +340,198 @@
             collective_id=1, has_side_effects=True, vmem_limit_bytes=40 * 1024 * 1024
         ),
         cost_estimate=pl.CostEstimate(
-            flops=64 * rows * width, bytes_accessed=64 * rows * width, transcendentals=0
+            flops=8192 * rows * width, bytes_accessed=4 * rows * width, transcendentals=0
         ),
         name="reduce_rows",
-    )(grads, small)
+    )(*operands, small)
+
+
+def line_copy(src, dst, sems, number, device):
+    return pltpu.make_async_remote_copy(
+        src_ref=src,
+        dst_ref=dst,
+        send_sem=sems[0].at[number],
+        recv_sem=sems[1].at[number],
+        device_id=device,
+        device_id_type=MESH,
+    )
+
+
+def plane_places():
+    e, z, step_core, chips = positions()
+    places = [(a, h, chips[a] + h * step_core) for a in range(4) for h in range(2)]
+    return e, z, chips, places[1:]
+
+
+def dispatch_kernel(
+    out_ref, full_ref, plane_send, plane_recv, up_send, up_recv, down_send, down_recv
+):
+    e, z, chips, places = plane_places()
+    greet([(d, z) for _, _, d in places] + [(e, lax.rem(z + t, 4)) for t in (1, 2, 3)])
+    lines = (((up_send, up_recv), 1), ((down_send, down_recv), -1))
+    pairs = [lax.div(chip, 2) * 2 for chip in chips]
+    plane = []
+    for a, h, device in places:
+        copy = line_copy(
+            out_ref.at[device], full_ref.at[z * 8 + e], (plane_send, plane_recv), a * 2 + h,
+            (device, z),
+        )
+        copy.start()
+        plane.append(copy)
+    full_ref[z * 8 + e] = out_ref[e]
+
+    def inside(depth):
+        return (depth >= 0) & (depth <= 3)
+
+    def hop(line, sign, step, a):
+        block = full_ref.at[pl.ds((z - sign * step) * 8 + pairs[a], 2)]
+        return line_copy(block, block, line, step * 4 + a, (e, z + sign))
+
+    def landed(line, sign, step, a):
+        block = full_ref.at[pl.ds((z - sign * (step + 1)) * 8 + pairs[a], 2)]
+        return line_copy(block, block, line, step * 4 + a, (e, z - sign))
+
+    for step in range(4):
+        for a in range(4):
+            if step == 0:
+                for copy, (chip, _, _) in zip(plane, places):
+                    if chip == a:
+                        copy.wait_recv()
+            for line, sign in lines:
+                if step > 0:
+
+                    @pl.when(inside(z - sign * step))
+                    def _(line=line, sign=sign, step=step, a=a):
+                        landed(line, sign, step - 1, a).wait_recv()
+
+                if step < 3:
+
+                    @pl.when(inside(z - sign * step) & inside(z + sign))
+                    def _(line=line, sign=sign, step=step, a=a):
+                        hop(line, sign, step, a).start()
+
+    for copy in plane:
+        copy.wait_send()
+    for step in range(3):
+        for line, sign in lines:
+
+            @pl.when(inside(z - sign * step) & inside(z + sign))
+            def _(line=line, sign=sign, step=step):
+                for a in range(4):
+                    hop(line, sign, step, a).wait_send()
+
+
+def return_kernel(
+    part_ref, back_ref, leaving, arriving, result,
+    plane_send, plane_recv, up_send, up_recv, down_send, down_recv,
+):
+    e, z, chips, places = plane_places()
+    greet([(d, z) for _, _, d in places] + [(e, lax.rem(z + t, 4)) for t in (1, 2, 3)])
+    lines = (((up_send, up_recv), 1), ((down_send, down_recv), -1))
+    pairs = [lax.div(chip, 2) * 2 for chip in chips]
+
+    def inside(depth):
+        return (depth >= 0) & (depth <= 3)
+
+    def hop(way, ahead, a):
+        line, sign = lines[way]
+        return line_copy(
+            leaving.at[way, ahead - 1, a], arriving.at[way, ahead - 1, a], line,
+            (ahead - 1) * 4 + a, (e, z + sign),
+        )
+
+    def landed(way, ahead, a):
+        line, sign = lines[way]
+        place = arriving.at[way, ahead, a]
+        line_copy(place, place, line, ahead * 4 + a, (e, z - sign)).wait_recv()
+        return place[...].astype(jnp.float32)
+
+    def own(depth, a):
+        return part_ref[pl.ds(depth * 8 + pairs[a], 2)]
+
+    for ahead in (3, 2, 1):
+        for a in (3, 1, 2, 0):
+            for way, (_, sign) in enumerate(lines):
+
+                @pl.when(inside(z + sign * ahead))
+                def _(way=way, sign=sign, ahead=ahead, a=a):
+                    leaving[way, ahead - 1, a] = own(z + sign * ahead, a)
+                    if ahead < 3:
+
+                        @pl.when(inside(z - sign))
+                        def _():
+                            value = own(z + sign * ahead, a).astype(jnp.float32)
+                            value = value + landed(way, ahead, a)
+                            leaving[way, ahead - 1, a] = value.astype(jnp.bfloat16)
+
+                    hop(way, ahead, a).start()
+
+    plane = []
+    for a in (3, 1, 2, 0):
+        result[a] = own(z, a).astype(jnp.float32)
+        for way, (_, sign) in enumerate(lines):
+
+            @pl.when(inside(z - sign))
+            def _(way=way, a=a):
+                result[a] = result[a] + landed(way, 0, a)
+
+        for core in range(2):
+            leaving[0, 3, a, core] = result[a, core].astype(jnp.bfloat16)
+        for chip, h, device in places:
+            if chip == a:
+                copy = line_copy(
+                    leaving.at[0, 3, a, lax.rem(device, 2)], back_ref.at[e],
+                    (plane_send, plane_recv), a * 2 + h, (device, z),
+                )
+                copy.start()
+                plane.append(copy)
+    back_ref[e] = leaving[0, 3, 0, lax.rem(e, 2)]
+    for copy in plane:
+        copy.wait_recv()
+    for copy in plane:
+        copy.wait_send()
+    for ahead in (3, 2, 1):
+        for way, (_, sign) in enumerate(lines):
+
+            @pl.when(inside(z + sign * ahead))
+            def _(way=way, ahead=ahead):
+                for a in range(4):
+                    hop(way, ahead, a).wait_send()
+
+
+def line_call(kernel, operand, blocks, scratch, number, name):
+    _, rows, width = operand.shape
+    vmem = pl.BlockSpec(memory_space=pltpu.VMEM)
+    return pl.pallas_call(
+        kernel,
+        out_shape=jax.ShapeDtypeStruct((blocks, rows, width), operand.dtype),
+        in_specs=[vmem],
+        out_specs=vmem,
+        scratch_shapes=scratch
+        + [pltpu.SemaphoreType.DMA((8,))] * 2
+        + [pltpu.SemaphoreType.DMA((12,))] * 4,
+        compiler_params=pltpu.CompilerParams(
+            collective_id=number, has_side_effects=True, vmem_limit_bytes=40 * 1024 * 1024
+        ),
+        cost_estimate=pl.CostEstimate(
+            flops=0, bytes_accessed=80 * rows * width, transcendentals=0
+        ),
+        name=name,
+    )(operand)
+
+
+def dispatch_rows(outgoing):
+    return line_call(dispatch_kernel, outgoing, 32, [], 2, "dispatch_rows")
+
+
+def return_rows(partial):
+    _, rows, width = partial.shape
+    scratch = [
+        pltpu.VMEM((2, 4, 4, 2, rows, width), partial.dtype),
+        pltpu.VMEM((2, 3, 4, 2, rows, width), partial.dtype),
+        pltpu.VMEM((4, 2, rows, width), jnp.float32),
+    ]
+    return line_call(return_kernel, partial, 8, scratch, 3, "return_rows")
 
 
 def local(
@@ -386,28 +615,36 @@
     )
     choose = routes == jnp.arange(expert_count, dtype=jnp.int32)[None, :]
     gate_prob = jnp.sum(jnp.where(choose, gate_probs, 0.0), axis=1, keepdims=True)
-    rank_index = jnp.cumsum(choose.astype(jnp.int32), axis=0) - 1
-    slot_index = jnp.sum(jnp.where(choose, rank_index, 0), axis=1)
-    slot_place = routes[:, 0] * capacity + slot_index
+    earlier = jnp.asarray(np.tril(np.ones((row_count, row_count)), -1), dtype=jnp.bfloat16)
+    rank_index = jnp.dot(earlier, choose.astype(jnp.bfloat16), preferred_element_type=jnp.float32)
+    slot_index = jnp.sum(jnp.where(choose, rank_index, 0.0), axis=1).astype(jnp.int32)
+    half_rows = local_count * capacity
+    group_place = routes[:, 0] // local_count * half_rows
+    slot_place = routes[:, 0] * capacity + slot_index + group_place
     dispatch = (
-        jnp.arange(expert_count * capacity, dtype=jnp.int32)[:, None] == slot_place[None, :]
+        jnp.arange(2 * group_count * half_rows, dtype=jnp.int32)[:, None]
+        == jnp.concatenate([slot_place, slot_place + half_rows])[None, :]
     ).astype(jnp.bfloat16)
     grad_out = cotangent.astype(jnp.float32)
     grad_picked = (gate_prob * grad_out).astype(jnp.bfloat16)
     outgoing = jnp.dot(
         dispatch,
-        jnp.concatenate([ffn_low, grad_picked], axis=1),
+        jnp.concatenate([ffn_low, grad_picked], axis=0),
         preferred_element_type=jnp.float32,
     ).astype(jnp.bfloat16)
-    outgoing = outgoing.reshape(group_count, local_count, capacity, 2 * model_width)
-    arrived = lax.all_to_all(outgoing, "exp", split_axis=0, concat_axis=0, tiled=True)
-    gathered = lax.all_gather(arrived[None], "dp", axis=0, tiled=True)
+    outgoing = outgoing.reshape(group_count, 2 * half_rows, model_width)
+    if direct:
+        gathered = dispatch_rows(outgoing)
+    else:
+        arrived = lax.all_to_all(outgoing, "exp", split_axis=0, concat_axis=0, tiled=True)
+        gathered = lax.all_gather(arrived, "dp", axis=0, tiled=True)
     slot_rows = dp_count * group_count * capacity
-    gathered = jnp.transpose(gathered, (2, 0, 1, 3, 4)).reshape(
-        local_count, slot_rows, 2 * model_width
-    )
-    expert_rows = gathered[:, :, :model_width]
-    grad_result = gathered[:, :, model_width:]
+    gathered = gathered.reshape(-1, 2, local_count, capacity, model_width)
+    gathered = jnp.transpose(gathered, (1, 2, 0, 3, 4)).reshape(
+        2, local_count, slot_rows, model_width
+    )
+    expert_rows = gathered[0]
+    grad_result = gathered[1]
     hidden_pre = jnp.einsum(
         "lsd,ldf->lsf", expert_rows, expert_in, preferred_element_type=jnp.float32
     )
@@ -425,33 +662,32 @@
     grad_expert_in = jnp.einsum(
         "lsd,lsf->ldf", expert_rows, grad_pre, preferred_element_type=jnp.float32
     )
-    partial = jnp.concatenate(
-        [partial_out.astype(jnp.bfloat16), grad_part.astype(jnp.bfloat16)], axis=2
-    ).reshape(local_count, dp_count, group_count, capacity, 2 * model_width)
-    partial = jnp.transpose(partial, (1, 2, 0, 3, 4))
-    result_rows = lax.psum_scatter(partial, "dp", scatter_dimension=0, tiled=True)[0]
-    returned = lax.all_to_all(result_rows, "exp", split_axis=0, concat_axis=0, tiled=True)
+    partial = jnp.stack(
+        [partial_out.astype(jnp.bfloat16), grad_part.astype(jnp.bfloat16)]
+    ).reshape(2, local_count, dp_count * group_count, capacity, model_width)
+    partial = jnp.transpose(partial, (2, 0, 1, 3, 4)).reshape(-1, 2 * half_rows, model_width)
+    if direct:
+        returned = return_rows(partial)
+    else:
+        result_rows = lax.psum_scatter(partial, "dp", scatter_dimension=0, tiled=True)
+        returned = lax.all_to_all(result_rows, "exp", split_axis=0, concat_axis=0, tiled=True)
     picked_both = lax.dot_general(
         dispatch,
-        returned.reshape(expert_count * capacity, 2 * model_width),
+        returned.reshape(-1, model_width),
         (((0,), (0,)), ((), ())),
         preferred_element_type=jnp.float32,
     )
-    picked = picked_both[:, :model_width]
-    grad_ffn = picked_both[:, model_width:]
+    picked = picked_both[:row_count]
+    grad_ffn = picked_both[row_count:]
     mixed = (middle + gate_prob * picked).astype(jnp.bfloat16)
     gate_grad = jnp.sum(grad_out * picked, axis=1, keepdims=True)
     logit_grad = (gate_probs * (jnp.where(choose, gate_grad, 0.0) - gate_prob * gate_grad)).astype(
         jnp.bfloat16
     )
     grad_ffn = grad_ffn + jnp.dot(logit_grad, full_route.T, preferred_element_type=jnp.float32)
-    grad_router = jnp.einsum("td,te->de", ffn_low, logit_grad, preferred_element_type=jnp.float32)
     grad_middle_norm, grad_gain_ffn = ffn_norm_pull(grad_ffn)
     grad_middle = grad_out + grad_middle_norm
     branch_grad = grad_middle.astype(jnp.bfloat16)
-    grad_attn_out = jnp.einsum(
-        "td,te->de", attended_low, branch_grad, preferred_element_type=jnp.float32
-    )
     grad_attended = jnp.dot(branch_grad, full_out.T, preferred_element_type=jnp.float32).astype(
         jnp.bfloat16
     )
@@ -491,34 +727,35 @@
         ],
         axis=1,
     ).astype(jnp.bfloat16)
-    grad_attn_qkv = jnp.einsum(
-        "td,tf->df", normed_low, grad_qkv, preferred_element_type=jnp.float32
-    )
     grad_normed = jnp.dot(grad_qkv, full_qkv.T, preferred_element_type=jnp.float32)
     grad_inputs_norm, grad_gain_attn = attn_norm_pull(grad_normed)
     grad_in = grad_middle + grad_inputs_norm
-    stacked = jnp.concatenate(
-        [
-            grad_attn_qkv.astype(jnp.bfloat16),
-            grad_attn_out.astype(jnp.bfloat16),
-            grad_router.astype(jnp.bfloat16),
-            jnp.zeros((model_width, full_width - dense_width), jnp.bfloat16),
-        ],
-        axis=1,
-    )
+    padded_logit = jnp.pad(logit_grad, ((0, 0), (0, full_width - dense_width)))
+    dense_pairs = ((normed_low, grad_qkv), (attended_low, branch_grad), (ffn_low, padded_logit))
     if direct:
         small = jnp.concatenate([grad_gain_attn, grad_gain_ffn, grad_bias.reshape(-1)])
         small_size = small.shape[0]
         small_rows = -(-small_size // (8 * lane_count)) * 8
         small = jnp.pad(small, (0, small_rows * lane_count - small_size))
         owned, small = reduce_rows(
-            stacked.reshape(-1, shard_rows, full_width), small.reshape(small_rows, lane_count)
+            [left.T for left, _ in dense_pairs] + [right for _, right in dense_pairs],
+            shard_rows,
+            small.reshape(small_rows, lane_count),
         )
         small = small.reshape(-1)
         grad_gain_attn = small[:model_width]
         grad_gain_ffn = small[model_width : 2 * model_width]
         grad_bias = small[2 * model_width : small_size].reshape(bucket_count, head_count)
     else:
+        stacked = jnp.concatenate(
+            [
+                jnp.einsum("td,te->de", left, right, preferred_element_type=jnp.float32).astype(
+                    jnp.bfloat16
+                )
+                for left, right in dense_pairs
+            ],
+            axis=1,
+        )
         pieces = lax.all_to_all(
             stacked.reshape(group_count, dp_count * shard_rows, full_width),
             "exp",

time: 299 us -> 232 us (0.78)
  waiting for transfers between devices: 83.5 us -> 0 us
  Pallas kernels: 78.6 us -> 142 us
  between operations: 14.9 us -> 1.45 us
  blocking collectives: 12.8 us -> 0 us
  local copies, waits for them, and re-layouts: 47.8 us -> 36.7 us
  starting transfers between devices: 4.62 us -> 0 us
  matrix products: 45 us -> 40.9 us
    pallas_call x0 -> x2, Pallas kernels: none -> 73.9 us  [line_call(): pl.pallas_call(kernel, out_shape=jax.ShapeDtypeStruct((blocks, rows, widt...]
    all_gather x1 -> x0, waiting for transfers between devices: 42.9 us -> none  [local(): gathered = lax.all_gather(arrived[None], 'dp', axis=0, tiled=True)]
    reduce_scatter x1 -> x0, waiting for transfers between devices: 40.4 us -> none  [local(): lax.psum_scatter(partial, 'dp', scatter_dimension=0, tiled=True)[0]]
    all_to_all x1 -> x0, blocking collectives: 12.8 us -> none  [local(): lax.all_to_all(outgoing, 'exp', split_axis=0, concat_axis=0, tiled=True)]
    pallas_call x1, Pallas kernels: 45.5 us -> 35.3 us  [reduce_rows(): pl.pallas_call(reduce_kernel, out_shape=(jax.ShapeDtypeStruct((rows, widt...]
    concatenate x2 -> x0, local copies, waits for them, and re-layouts: 9.91 us -> none  [the longest x1 7.89 us: local(): jnp.concatenate([grad_attn_qkv.astype(jnp.bfloat16), grad_attn_out.astype...]
    dot_general x5 -> x3, matrix products: 8.14 us -> 2.72 us  [the longest x1 1.21 us: local(): jnp.dot(dispatch, jnp.concatenate([ffn_low, grad_picked], axis=0), prefer...]
    all_to_all x1 -> x0, starting transfers between devices: 4.36 us -> none  [local(): lax.all_to_all(result_rows, 'exp', split_axis=0, concat_axis=0, tiled=True)]
  transfers between devices with their start and end apart: 3 -> 0, of which waited for: 3 -> 0; matrix products, arithmetic and copies ran while one was open for 3% -> 0% of each run, Pallas kernels for 0% -> 0%
where the time goes in v2:
time: 232 us; the launch traced here: 231 us
  Pallas kernels  142 us (61%)
  matrix products  40.9 us (18%)
  local copies, waits for them, and re-layouts  36.7 us (16%)
  other arithmetic  9.91 us (4%)
    pallas_call x2, Pallas kernels, line_call(): pl.pallas_call(kernel, out_shape=jax.ShapeDtypeStruct((blocks, rows, widt...  73.9 us
    pallas_call x1, Pallas kernels, reduce_rows(): pl.pallas_call(reduce_kernel, out_shape=(jax.ShapeDtypeStruct((rows, widt...  35.3 us
    pallas_call x1, Pallas kernels, gather_rows(): pl.pallas_call(gather_kernel, out_shape=jax.ShapeDtypeStruct((32, rows, w...  33.2 us
    unnamed x104, local copies, waits for them, and re-layouts  11.7 us
    dot_general x1, matrix products, local(): jnp.einsum('lsd,lsf->ldf', expert_rows, grad_pre, preferred_element_type=...  5.27 us

profile of v2, /device:TPU:0, one launch (start us, length us, event | category | flops | bytes accessed | tf_op | source)
XLA Modules:
  0.0 231.3 jit_solution(14941158248848982506)
XLA Ops:
  0.7 0.9 copy.82
  1.6 1.6 concatenate.17.mine_ref
  3.2 33.2 %gather_rows.1 = bf16[32,24,3200]{2,1,0:T(8,128)(2,1)} custom-call(bf16[24,3200]{1,0:T(8,128)(2,1)} %concatenate.17.mine_ref), custom_call_target="tpu_custom_call" | custom-call | bytes 4915200 | tf_op jit(solution)/shard_map/gather_rows/pallas_call | solution.py:153
  36.5 0.6 copy-done.43
  37.6 2.7 %convolution_convert_fusion = bf16[128,2304]{1,0:T(8,128)(2,1)S(1)} fusion(bf16[768,3200]{1,0:T(8,128)(2,1)} %bitcast.84, bf16[128,768]{1,0:T(8,128)(2,1)S(1)} %copy-done.18, f32[768]{0:T(1024)S(1)} %copy-done.36, f32[128]{0:T(128)S(1)} %fusion.55), kind=kOutput, calls=%fused_computation | convolution fusion | flops 453672960 | bytes 4328960 | tf_op jit(solution)/shard_map/dot_general | solution.py:583
  40.3 0.7 fusion.60
  41.1 0.8 copy.83
  41.9 1.8 fusion.63
  43.9 1.1 copy.86
  45.3 1.2 copy.85
  46.8 1.5 fusion.61
  48.5 1.2 convolution_convert_fusion.6
  49.8 1.7 multiply_reduce_fusion.3
  51.5 0.7 copy-done.5
  52.4 0.7 copy-done.27
  53.0 1.8 fusion.62
  54.8 1.4 copy.88
  56.2 1.0 fusion.49
  57.2 1.1 select_reduce_fusion
  58.4 1.1 fusion.14
  59.5 0.7 broadcast_add_fusion
  60.2 1.2 convolution_convert_fusion.3
  61.4 39.1 %dispatch_rows.1 = bf16[32,40,768]{2,1,0:T(8,128)(2,1)S(1)} custom-call(bf16[8,40,768]{2,1,0:T(8,128)(2,1)S(1)} %bitcast.81), custom_call_target="tpu_custom_call" | custom-call | bytes 2457600 | tf_op jit(solution)/shard_map/dispatch_rows/pallas_call | solution.py:505
  101.1 1.0 copy.91
  102.2 0.9 fusion.25
  103.1 1.0 copy.94
  104.4 1.9 fusion.9
  106.3 1.0 convolution_convert_fusion.1
  107.3 1.0 copy.96
  108.3 1.3 convolution_convert_fusion.2
  109.6 1.0 copy.93
  110.6 2.8 %maximum_bitcast_fusion = bf16[32,2,2,10,768]{4,2,3,0,1:T(2,128)(2,1)S(1)} fusion(bf16[1,2,32,10,768]{4,1,3,2,0:T(2,128)(2,1)S(1)} %bitcast.93, bf16[1,2,32,10,768]{4,1,3,2,0:T(2,128)(2,1)S(1)} %bitcast.94), kind=kLoop, calls=%fused_computation.13 | loop fusion | flops 983040 | bytes 3932160 | tf_op jit(solution)/shard_map/transpose | solution.py:668
  113.7 1.1 copy.98.part_ref
  114.9 34.7 %return_rows.1 = bf16[8,40,768]{2,1,0:T(8,128)(2,1)S(1)} custom-call(bf16[32,40,768]{2,1,0:T(8,128)(2,1)S(1)} %copy.98.part_ref), custom_call_target="tpu_custom_call" | custom-call | bytes 2457600 | tf_op jit(solution)/shard_map/return_rows/pallas_call | solution.py:505
  150.1 0.8 fusion.33
  151.1 1.3 multiply_reduce_fusion.1
  153.1 2.5 %convolution_convert_fusion.5 = bf16[128,768]{1,0:T(8,128)(2,1)} fusion(bf16[128,768]{1,0:T(8,128)(2,1)S(1)} %fusion.58.branch_ref, bf16[768,3200]{1,0:T(8,128)(2,1)} %bitcast.88), kind=kOutput, calls=%fused_computation.26 | convolution fusion | flops 151093248 | bytes 1572864 | tf_op jit(solution)/shard_map/dot_general | solution.py:691
  155.6 0.7 copy-done.3
  156.3 1.8 copy.99
  158.1 2.0 convolution_convert_fusion.4
  160.1 1.8 copy.105
  161.8 1.4 multiply_reduce_fusion
  163.4 0.7 copy-done.11
  164.5 0.8 copy.104
  165.4 1.3 fusion.12
  166.7 0.8 copy.103
  167.6 4.2 %fusion.31 = (f32[768]{0:T(1024)}, f32[128]{0:T(128)S(1)}, f32[128,768]{1,0:T(8,128)S(1)}) fusion(bf16[128,768]{1,0:T(8,128)(2,1)S(1)} %copy-done.20, f32[128]{0:T(128)} %copy-done.41, f32[768]{0:T(1024)S(1)} %copy-done.37, bf16[768,3200]{1,0:T(8,128)(2,1)} %bitcast.89, bf16[128,768]{1,0:T(8,128)(2,1)S(1)} %copy-done.26, bf16[128,768]{1,0:T(8,128)(2,1)} %copy.104, ...), kind=kOutput, calls=%fused_computation.60 | convolution fusion | flops 455441536 | bytes 4725760 | tf_op jit(solution)/shard_map/dot_general | solution.py:730
  171.9 1.1 fusion.50
  173.0 1.8 copy.108.normed_ref
  174.9 0.8 copy.109.ffn_ref
  175.7 1.1 pad_maximum_fusion.qkv_ref
  176.8 1.9 copy.106
  178.7 1.1 pad.25
  180.8 0.9 copy-done.1
  181.7 0.9 copy-done.2
  182.6 0.9 copy-done.4
  183.6 35.3 %reduce_rows.1 = (f32[24,3200]{1,0:T(8,128)S(1)}, f32[16,128]{1,0:T(8,128)S(1)}) custom-call(bf16[768,128]{1,0:T(8,128)(2,1)S(1)} %copy-done.1, bf16[768,128]{1,0:T(8,128)(2,1)S(1)} %bitcast.80, bf16[768,128]{1,0:T(8,128)(2,1)S(1)} %copy-done.2, bf16[128,2304]{1,0:T(8,128)(2,1)S(1)} %pad_maximum_fusion.qkv_ref, bf16[128,768]{1,0:T(8,128)(2,1)S(1)} %copy-done.4, ...), custom_call_target="tpu_custom_call" | custom-call | flops 629145600 | bytes 307200 | tf_op jit(solution)/shard_map/reduce_rows/pallas_call | solution.py:315
  218.9 0.6 slice_bitcast_fusion
  219.5 0.7 slice.69
  220.2 0.6 slice.70
  220.9 0.7 copy.112
  221.6 0.7 copy.113
  222.3 5.3 %fusion.23 = f32[2,768,768]{2,1,0:T(8,128)} fusion(bf16[2,320,768]{2,1,0:T(8,128)(2,1)} %copy-done.25, bf16[2,320,768]{2,0,1:T(2,128)(2,1)} %bitcast.83), kind=kOutput, calls=%fused_computation.38 | convolution fusion | flops 754974720 | bytes 6684672 | tf_op jit(solution)/shard_map/lsd,lsf->ldf/dot_general | solution.py:662
  227.6 3.8 %fusion.17 = f32[2,768,768]{2,1,0:T(8,128)} fusion(bf16[2,320,768]{2,0,1:T(2,128)(2,1)S(1)} %bitcast.96, f32[2,320,768]{2,1,0:T(8,128)S(1)} %copy-done.10), kind=kOutput, calls=%fused_computation.34 | convolution fusion | flops 759398400 | bytes 7667712 | tf_op jit(solution)/shard_map/lsf,lsd->lfd/dot_general | solution.py:659
  (125 shorter events, 6.1 us)
Async XLA Ops:
  0.6 101.5 %copy-start = (bf16[2,768,768]{2,1,0:T(8,128)(2,1)S(1)}, bf16[2,768,768]{2,1,0:T(8,128)(2,1)}, u32[]{:S(2)}) copy-start(bf16[2,768,768]{2,1,0:T(8,128)(2,1)} %param.24) | copy-start | bytes 7077892
  3.2 33.2 %copy-start.18 = (bf16[128,768]{1,0:T(8,128)(2,1)S(1)}, bf16[128,768]{1,0:T(8,128)(2,1)}, u32[]{:S(2)}) copy-start(bf16[128,768]{1,0:T(8,128)(2,1)} %param.14) | copy-start | bytes 589828
  3.2 34.4 %copy-start.36 = (f32[768]{0:T(1024)S(1)}, f32[768]{0:T(1024)}, u32[]{:S(2)}) copy-start(f32[768]{0:T(1024)} %param.18) | copy-start | bytes 9220
  36.5 0.6 copy-start.43
  37.1 0.5 copy-start.41
  37.6 4.2 %copy-start.34 = (f32[32,12]{0,1:T(8,128)S(1)}, f32[32,12]{0,1:T(8,128)}, u32[]{:S(2)}) copy-start(f32[32,12]{0,1:T(8,128)} %param.21) | copy-start | bytes 4612
  43.9 2.6 %copy-start.48 = (s32[1,3]{1,0:T(1,128)S(1)}, s32[1,3]{1,0:T(1,128)}, u32[]{:S(2)}) copy-start(s32[1,3]{1,0:T(1,128)} %param.16) | copy-start | bytes 40
  45.3 3.2 %copy-start.22 = (bf16[128,768]{0,1:T(8,128)(2,1)}, bf16[128,768]{0,1:T(8,128)(2,1)S(1)}, u32[]{:S(2)}) copy-start(bf16[128,768]{0,1:T(8,128)(2,1)S(1)} %copy.84) | copy-start | bytes 589828
  46.4 2.1 copy-start.21
  46.8 2.9 %copy-start.19 = (bf16[128,768]{1,0:T(8,128)(2,1)S(1)}, bf16[128,768]{1,0:T(8,128)(2,1)}, u32[]{:S(2)}) copy-start(bf16[128,768]{1,0:T(8,128)(2,1)} %param.14) | copy-start | bytes 589828
  48.3 3.9 %copy-start.30 = (f32[768]{0:T(1024)S(1)}, f32[768]{0:T(1024)}, u32[]{:S(2)}) copy-start(f32[768]{0:T(1024)} %param.22) | copy-start | bytes 9220
  48.5 9.8 %copy-start.17 = (bf16[128,768]{1,0:T(8,128)(2,1)S(1)}, bf16[128,768]{1,0:T(8,128)(2,1)}, u32[]{:S(2)}) copy-start(bf16[128,768]{1,0:T(8,128)(2,1)} %param.15) | copy-start | bytes 589828
  51.5 0.8 copy-start.5
  51.5 3.3 %copy-start.45 = (f32[128]{0:T(128)}, f32[128]{0:T(128)S(1)}, u32[]{:S(2)}) copy-start(f32[128]{0:T(128)S(1)} %get-tuple-element.63) | copy-start | bytes 1540
  52.2 2.5 %copy-start.31 = (f32[128]{0:T(128)}, f32[128]{0:T(128)S(1)}, u32[]{:S(2)}) copy-start(f32[128]{0:T(128)S(1)} %fusion.56) | copy-start | bytes 1540
  52.4 0.7 copy-start.27
  102.1 1.0 copy-start.8
  102.2 2.3 copy-start.47
  103.1 5.2 %copy-start.9 = (f32[2,320,768]{2,1,0:T(8,128)}, f32[2,320,768]{2,1,0:T(8,128)S(1)}, u32[]{:S(2)}) copy-start(f32[2,320,768]{2,1,0:T(8,128)S(1)} %fusion.25) | copy-start | bytes 5898244
  104.1 2.2 copy-start.13
  106.3 1.0 copy-start.25
  114.8 35.2 %copy-start.6 = (f32[128,768]{1,0:T(8,128)S(1)}, f32[128,768]{1,0:T(8,128)}, u32[]{:S(2)}) copy-start(f32[128,768]{1,0:T(8,128)} %copy-done.5) | copy-start | bytes 1179652
  114.8 36.0 %copy-start.24 = (f32[128,16]{1,0:T(8,128)S(1)}, f32[128,16]{1,0:T(8,128)}, u32[]{:S(2)}) copy-start(f32[128,16]{1,0:T(8,128)} %copy.88) | copy-start | bytes 24580
  114.9 36.0 %copy-start.35 = (s32[128,1]{0,1:T(1,128)S(1)}, s32[128,1]{0,1:T(1,128)}, u32[]{:S(2)}) copy-start(s32[128,1]{0,1:T(1,128)} %param.17) | copy-start | bytes 1540
  114.9 36.2 %copy-start.32 = (f32[128]{0:T(128)S(1)}, f32[128]{0:T(128)}, u32[]{:S(2)}) copy-start(f32[128]{0:T(128)} %copy-done.31) | copy-start | bytes 1540
  149.6 2.7 %copy-start.46 = (f32[128]{0:T(128)S(1)}, f32[128]{0:T(128)}, u32[]{:S(2)}) copy-start(f32[128]{0:T(128)} %copy-done.45) | copy-start | bytes 1540
  151.1 1.3 copy-start.28
  152.3 0.8 copy-start.15
  152.4 0.8 copy-start.39
  155.6 0.7 copy-start.3
  161.8 2.3 %copy-start.23 = (bf16[128,768]{0,1:T(8,128)(2,1)S(1)}, bf16[128,768]{0,1:T(8,128)(2,1)}, u32[]{:S(2)}) copy-start(bf16[128,768]{0,1:T(8,128)(2,1)} %copy-done.22) | copy-start | bytes 589828
  163.4 0.7 copy-start.11
  164.2 3.4 %copy-start.20 = (bf16[128,768]{1,0:T(8,128)(2,1)S(1)}, bf16[128,768]{1,0:T(8,128)(2,1)}, u32[]{:S(2)}) copy-start(bf16[128,768]{1,0:T(8,128)(2,1)} %param.14) | copy-start | bytes 589828
  164.2 3.4 %copy-start.26 = (bf16[128,768]{1,0:T(8,128)(2,1)S(1)}, bf16[128,768]{1,0:T(8,128)(2,1)}, u32[]{:S(2)}) copy-start(bf16[128,768]{1,0:T(8,128)(2,1)} %copy.105) | copy-start | bytes 589828
  164.2 3.4 %copy-start.37 = (f32[768]{0:T(1024)S(1)}, f32[768]{0:T(1024)}, u32[]{:S(2)}) copy-start(f32[768]{0:T(1024)} %param.18) | copy-start | bytes 9220
  167.5 4.3 %copy-start.44 = (f32[128]{0:T(128)S(1)}, f32[128]{0:T(128)}, u32[]{:S(2)}) copy-start(f32[128]{0:T(128)} %copy-done.43) | copy-start | bytes 1540
  167.6 4.3 %copy-start.7 = (f32[128,768]{1,0:T(8,128)S(1)}, f32[128,768]{1,0:T(8,128)}, u32[]{:S(2)}) copy-start(f32[128,768]{1,0:T(8,128)} %copy-done.5) | copy-start | bytes 1179652
  167.6 4.3 %copy-start.16 = (f32[128,768]{1,0:T(8,128)S(1)}, f32[128,768]{1,0:T(8,128)}, u32[]{:S(2)}) copy-start(f32[128,768]{1,0:T(8,128)} %copy-done.15) | copy-start | bytes 1179652
  167.6 4.3 %copy-start.33 = (f32[128]{0:T(128)S(1)}, f32[128]{0:T(128)}, u32[]{:S(2)}) copy-start(f32[128]{0:T(128)} %copy-done.31) | copy-start | bytes 1540
  167.6 4.3 %copy-start.40 = (f32[128]{0:T(128)S(1)}, f32[128]{0:T(128)}, u32[]{:S(2)}) copy-start(f32[128]{0:T(128)} %copy-done.39) | copy-start | bytes 1540
  167.6 4.3 %copy-start.42 = (f32[128]{0:T(128)S(1)}, f32[128]{0:T(128)}, u32[]{:S(2)}) copy-start(f32[128]{0:T(128)} %copy-done.41) | copy-start | bytes 1540
  173.0 3.8 %copy-start.29 = (bf16[128,16]{1,0:T(8,128)(2,1)S(1)}, bf16[128,16]{1,0:T(8,128)(2,1)}, u32[]{:S(2)}) copy-start(bf16[128,16]{1,0:T(8,128)(2,1)} %copy-done.28) | copy-start | bytes 12292
  178.7 1.5 copy-start.12
  178.7 2.0 copy-start.38
  180.8 0.9 copy-start.1
  181.7 0.9 copy-start.2
  182.6 0.9 copy-start.4
  222.3 5.3 %copy-start.10 = (f32[2,320,768]{2,1,0:T(8,128)S(1)}, f32[2,320,768]{2,1,0:T(8,128)}, u32[]{:S(2)}) copy-start(f32[2,320,768]{2,1,0:T(8,128)} %copy-done.9) | copy-start | bytes 5898244
  222.3 5.3 %copy-start.14 = (bf16[1,2,32,10,768]{4,1,3,2,0:T(2,128)(2,1)S(1)}, bf16[1,2,32,10,768]{4,1,3,2,0:T(2,128)(2,1)}, u32[]{:S(2)}) copy-start(bf16[1,2,32,10,768]{4,1,3,2,0:T(2,128)(2,1)} %copy-done.13) | copy-start | bytes 2949124

commit v3 on v2

--- a/solution.py
+++ b/solution.py
@@ -45,15 +45,6 @@
     boundary = jnp.cumsum(lengths, axis=-1)
     position = jnp.arange(row_count, dtype=jnp.int32)
     return jnp.sum((position[:, None] >= boundary[..., None, :]).astype(jnp.int32), axis=-1)
-
-
-def score_block(queries, key_rows, pos_bias, allowed, score_scale):
-    scores = (
-        jnp.einsum("qhe,khe->hqk", queries, key_rows, preferred_element_type=jnp.float32)
-        * score_scale
-        + pos_bias
-    )
-    return jnp.where(allowed, scores, -1e30)
 
 
 def positions():
@@ -534,6 +525,88 @@
     return line_call(return_kernel, partial, 8, scratch, 3, "return_rows")
 
 
+def contract(left, right, left_axis, right_axis):
+    return lax.dot_general(
+        left, right, (((left_axis,), (right_axis,)), ((), ())), preferred_element_type=jnp.float32
+    )
+
+
+def attend_kernel(
+    head_count, head_size, qkv_ref, column_ref, row_ref, offset_ref, out_ref, probs_ref
+):
+    rows = qkv_ref.shape[0]
+    width = head_count * head_size
+    allowed = column_ref[...] == row_ref[...]
+    for pair in range(0, head_count, 2):
+        halves = []
+        for h in (pair, pair + 1):
+            queries, keys, values = (
+                qkv_ref[:, part * width + h * head_size : part * width + (h + 1) * head_size]
+                for part in range(3)
+            )
+            bias = jnp.broadcast_to(offset_ref[h : h + 1, :], (rows, 2 * rows))
+            bias = pltpu.roll(bias, 0, 1, stride=1, stride_axis=0)[:, :rows]
+            scores = contract(queries, keys, 1, 1) * head_size ** (-0.5) + bias
+            scores = jnp.where(allowed, scores, -1e30)
+            weights = jnp.exp(scores - jnp.max(scores, axis=-1, keepdims=True))
+            probs = weights / jnp.sum(weights, axis=-1, keepdims=True)
+            probs_ref[h] = probs
+            halves.append(contract(probs.astype(jnp.bfloat16), values, 1, 0))
+        out_ref[:, pair * head_size : (pair + 2) * head_size] = jnp.concatenate(
+            halves, axis=1
+        ).astype(jnp.bfloat16)
+
+
+def attend_back_kernel(
+    head_count, head_size, qkv_ref, probs_ref, grad_ref, flip_ref, out_ref, offset_ref
+):
+    rows = qkv_ref.shape[0]
+    width = head_count * head_size
+    scale = head_size ** (-0.5)
+    line = lax.broadcasted_iota(jnp.int32, (rows, rows), 0)
+    lane = lax.broadcasted_iota(jnp.int32, (rows, rows), 1)
+    for pair in range(0, head_count, 2):
+        halves = []
+        for h in (pair, pair + 1):
+            queries, keys, values = (
+                qkv_ref[:, part * width + h * head_size : part * width + (h + 1) * head_size]
+                for part in range(3)
+            )
+            grad = grad_ref[:, h * head_size : (h + 1) * head_size]
+            probs = probs_ref[h]
+            grad_probs = contract(grad, values, 1, 1)
+            inner = jnp.sum(probs * grad_probs, axis=-1, keepdims=True)
+            scores = (probs * (grad_probs - inner)).astype(jnp.bfloat16)
+            halves.append(
+                (
+                    contract(scores, keys, 1, 0) * scale,
+                    contract(scores, queries, 0, 0) * scale,
+                    contract(probs.astype(jnp.bfloat16), grad, 0, 0),
+                )
+            )
+            turned = pltpu.roll(contract(flip_ref[...], scores, 1, 0), 1, 1, stride=1, stride_axis=0)
+            ahead = jnp.where(lane <= line, turned, 0.0)
+            offset_ref[h : h + 1, :rows] = jnp.sum(ahead, axis=0, keepdims=True)
+            offset_ref[h : h + 1, rows:] = jnp.sum(turned - ahead, axis=0, keepdims=True)
+        for part in range(3):
+            start = part * width + pair * head_size
+            out_ref[:, start : start + 2 * head_size] = jnp.concatenate(
+                [halves[0][part], halves[1][part]], axis=1
+            ).astype(jnp.bfloat16)
+
+
+def attention_call(kernel, shapes, operands, name):
+    vmem = pl.BlockSpec(memory_space=pltpu.VMEM)
+    return pl.pallas_call(
+        kernel,
+        out_shape=shapes,
+        in_specs=[vmem] * len(operands),
+        out_specs=tuple(vmem for _ in shapes),
+        compiler_params=pltpu.CompilerParams(vmem_limit_bytes=32 * 1024 * 1024),
+        name=name,
+    )(*operands)
+
+
 def local(
     hidden_in,
     cotangent,
@@ -551,7 +624,6 @@
     row_count, model_width = hidden_in.shape
     bucket_count, head_count = rel_bias.shape
     head_size = model_width // head_count
-    score_scale = head_size ** (-0.5)
     expert_count = router.shape[1]
     group_count = lax.axis_size("exp")
     local_count = expert_in.shape[0]
@@ -581,32 +653,22 @@
     normed, attn_norm_pull = jax.vjp(rms_norm, inputs, gain_attn)
     normed_low = normed.astype(jnp.bfloat16)
     qkv_low = jnp.dot(normed_low, full_qkv, preferred_element_type=jnp.float32).astype(jnp.bfloat16)
-    queries = qkv_low[:, :model_width].reshape(row_count, head_count, head_size)
-    key_rows = qkv_low[:, model_width : 2 * model_width].reshape(row_count, head_count, head_size)
-    value_rows = qkv_low[:, 2 * model_width :].reshape(row_count, head_count, head_size)
-    bucket_ids = bucket_table(row_count, bucket_count)
+    offset_table = bucket_table(row_count, bucket_count)
+    offset_bucket = np.concatenate([offset_table[0], offset_table[:, 0][:1], offset_table[:0:-1, 0]])
     bucket_hot = jnp.asarray(
-        bucket_ids.reshape(1, -1) == np.arange(bucket_count)[:, None], dtype=jnp.bfloat16
-    )
-    pos_bias = jnp.einsum(
-        "bh,bn->hn",
-        rel_bias,
-        bucket_hot.astype(jnp.float32),
-        precision=lax.Precision.HIGHEST,
-    ).reshape(head_count, row_count, row_count)
+        offset_bucket[:, None] == np.arange(bucket_count)[None, :], dtype=jnp.float32
+    )
+    offset_bias = jnp.einsum("nb,bh->hn", bucket_hot, rel_bias, precision=lax.Precision.HIGHEST)
     segment = segment_ids(lengths, row_count)[0]
-    allowed = (segment[:, None] == segment[None, :])[None]
-    scores = score_block(queries, key_rows, pos_bias, allowed, score_scale)
-    row_max = jnp.max(scores, axis=-1, keepdims=True)
-    log_total = row_max + jnp.log(jnp.sum(jnp.exp(scores - row_max), axis=-1, keepdims=True))
-    attn_probs = jnp.exp(scores - log_total)
-    attended = jnp.einsum(
-        "hqk,khe->qhe",
-        attn_probs.astype(jnp.bfloat16),
-        value_rows,
-        preferred_element_type=jnp.float32,
-    )
-    attended_low = attended.reshape(row_count, model_width).astype(jnp.bfloat16)
+    attended_low, attn_probs = attention_call(
+        functools.partial(attend_kernel, head_count, head_size),
+        (
+            jax.ShapeDtypeStruct((row_count, model_width), jnp.bfloat16),
+            jax.ShapeDtypeStruct((head_count, row_count, row_count), jnp.float32),
+        ),
+        (qkv_low, segment[:, None], segment[None, :], offset_bias),
+        "attend",
+    )
     middle = inputs + jnp.dot(attended_low, full_out, preferred_element_type=jnp.float32)
     ffn_norm, ffn_norm_pull = jax.vjp(rms_norm, middle, gain_ffn)
     ffn_low = ffn_norm.astype(jnp.bfloat16)
@@ -691,42 +753,21 @@
     grad_attended = jnp.dot(branch_grad, full_out.T, preferred_element_type=jnp.float32).astype(
         jnp.bfloat16
     )
-    grad_attended = grad_attended.reshape(row_count, head_count, head_size)
-    scores = score_block(queries, key_rows, pos_bias, allowed, score_scale)
-    attn_probs = jnp.exp(scores - log_total)
-    grad_values = jnp.einsum(
-        "hqk,qhe->khe",
-        attn_probs.astype(jnp.bfloat16),
-        grad_attended,
-        preferred_element_type=jnp.float32,
-    )
-    grad_probs = jnp.einsum(
-        "qhe,khe->hqk", grad_attended, value_rows, preferred_element_type=jnp.float32
-    )
-    inner_sum = jnp.sum(attn_probs * grad_probs, axis=-1, keepdims=True)
-    grad_scores = (attn_probs * (grad_probs - inner_sum)).astype(jnp.bfloat16)
-    grad_queries = (
-        jnp.einsum("hqk,khe->qhe", grad_scores, key_rows, preferred_element_type=jnp.float32)
-        * score_scale
-    )
-    grad_keys = (
-        jnp.einsum("hqk,qhe->khe", grad_scores, queries, preferred_element_type=jnp.float32)
-        * score_scale
-    )
-    grad_bias = jnp.einsum(
-        "bn,hn->bh",
-        bucket_hot,
-        grad_scores.reshape(head_count, row_count * row_count),
-        preferred_element_type=jnp.float32,
-    )
-    grad_qkv = jnp.concatenate(
-        [
-            grad_queries.reshape(row_count, model_width),
-            grad_keys.reshape(row_count, model_width),
-            grad_values.reshape(row_count, model_width),
-        ],
-        axis=1,
-    ).astype(jnp.bfloat16)
+    grad_qkv, offset_grad = attention_call(
+        functools.partial(attend_back_kernel, head_count, head_size),
+        (
+            jax.ShapeDtypeStruct((row_count, 3 * model_width), jnp.bfloat16),
+            jax.ShapeDtypeStruct((head_count, 2 * row_count), jnp.float32),
+        ),
+        (
+            qkv_low,
+            attn_probs,
+            grad_attended,
+            jnp.asarray(np.eye(row_count)[::-1], dtype=jnp.bfloat16),
+        ),
+        "attend_back",
+    )
+    grad_bias = jnp.einsum("nb,hn->bh", bucket_hot, offset_grad, precision=lax.Precision.HIGHEST)
     grad_normed = jnp.dot(grad_qkv, full_qkv.T, preferred_element_type=jnp.float32)
     grad_inputs_norm, grad_gain_attn = attn_norm_pull(grad_normed)
     grad_in = grad_middle + grad_inputs_norm

time: 232 us -> 209 us (0.901)
  local copies, waits for them, and re-layouts: 36.7 us -> 19.1 us
  matrix products: 40.9 us -> 27.1 us
  Pallas kernels: 142 us -> 150 us
    dot_general x8 -> x2, matrix products: 9.98 us -> 1.44 us  [the longest x1 1.24 us: local(): jnp.einsum('nb,hn->bh', bucket_hot, offset_grad, precision=lax.Precision....]
    pallas_call x0 -> x2, Pallas kernels: none -> 7.73 us  [attention_call(): pl.pallas_call(kernel, out_shape=shapes, in_specs=[vmem] * len(operands),...]
    reshape x5 -> x0, local copies, waits for them, and re-layouts: 4.62 us -> none  [the longest x1 1.77 us: local(): grad_values.reshape(row_count, model_width)]
    unnamed x104 -> x89, local copies, waits for them, and re-layouts: 11.7 us -> 7.93 us
    convert_element_type x2 -> x0, local copies, waits for them, and re-layouts: 3.66 us -> none  [the longest x1 1.91 us: local(): grad_scores = (attn_probs * (grad_probs - inner_sum)).astype(jnp.bfloat16)]
    dot_general x1, matrix products: 4.24 us -> 1.39 us  [local(): jnp.dot(grad_qkv, full_qkv.T, preferred_element_type=jnp.float32)]
    slice x4 -> x0, local copies, waits for them, and re-layouts: 2.85 us -> none  [the longest x2 1.87 us: local(): qkv_low[:, model_width:2 * model_width]]
where the time goes in v3:
time: 209 us; the launch traced here: 208 us
  Pallas kernels  150 us (72%)
  matrix products  27.1 us (13%)
  local copies, waits for them, and re-layouts  19.1 us (9%)
  other arithmetic  10.3 us (5%)
    pallas_call x2, Pallas kernels, line_call(): pl.pallas_call(kernel, out_shape=jax.ShapeDtypeStruct((blocks, rows, widt...  73.9 us
    pallas_call x1, Pallas kernels, reduce_rows(): pl.pallas_call(reduce_kernel, out_shape=(jax.ShapeDtypeStruct((rows, widt...  35.3 us
    pallas_call x1, Pallas kernels, gather_rows(): pl.pallas_call(gather_kernel, out_shape=jax.ShapeDtypeStruct((32, rows, w...  33.2 us
    unnamed x89, local copies, waits for them, and re-layouts  7.93 us
    pallas_call x2, Pallas kernels, attention_call(): pl.pallas_call(kernel, out_shape=shapes, in_specs=[vmem] * len(operands),...  7.73 us
    dot_general x1, matrix products, local(): jnp.einsum('lsd,lsf->ldf', expert_rows, grad_pre, preferred_element_type=...  5.27 us

profile of v3, /device:TPU:0, one launch (start us, length us, event | category | flops | bytes accessed | tf_op | source)
XLA Modules:
  0.0 208.0 jit_solution(10232580943615293538)
XLA Ops:
  0.7 0.9 copy.59
  1.6 1.6 concatenate.13.mine_ref
  3.2 33.2 %gather_rows.1 = bf16[32,24,3200]{2,1,0:T(8,128)(2,1)} custom-call(bf16[24,3200]{1,0:T(8,128)(2,1)} %concatenate.13.mine_ref), custom_call_target="tpu_custom_call" | custom-call | bytes 4915200 | tf_op jit(solution)/shard_map/gather_rows/pallas_call | solution.py:144
  36.4 0.1 fusion.30
  36.5 0.5 copy-done.35
  37.1 2.7 %convolution_convert_fusion.qkv_ref = bf16[128,2304]{1,0:T(8,128)(2,1)S(1)} fusion(bf16[768,3200]{1,0:T(8,128)(2,1)} %bitcast.58, bf16[128,768]{1,0:T(8,128)(2,1)S(1)} %copy-done.17, f32[768]{0:T(1024)S(1)} %copy-done.31, f32[128]{0:T(128)S(1)} %fusion.48), kind=kOutput, calls=%fused_computation | convolution fusion | flops 453672960 | bytes 4328960 | tf_op jit(solution)/shard_map/dot_general | solution.py:655
  39.8 0.2 reduce_window_sum.11
  40.1 0.1 copy.60.column_ref
  40.2 0.2 convolution_bitcast_fusion.offset_ref
  40.5 4.3 %attend.1 = (bf16[128,768]{1,0:T(8,128)(2,1)S(1)}, f32[12,128,128]{2,1,0:T(8,128)S(1)}) custom-call(bf16[128,2304]{1,0:T(8,128)(2,1)S(1)} %convolution_convert_fusion.qkv_ref, s32[128,1]{1,0:T(8,128)S(1)} %copy.60.column_ref, s32[1,128]{1,0:T(1,128)S(1)} %bitcast.53, f32[12,256]{1,0:T(8,128)S(1)} %convolution_bitcast_fusion.offset_ref), custom_call_target="tpu_custom_call" | custom-call | tf_op jit(solution)/shard_map/attend/pallas_call | solution.py:600
  44.8 0.9 copy-done.1
  45.7 1.7 multiply_reduce_fusion.2
  47.4 0.5 copy-done.39
  48.0 0.7 copy-done.19
  48.7 1.7 fusion.53
  50.4 0.7 copy.61
  51.1 1.0 fusion.42
  52.1 1.0 select_reduce_fusion
  53.2 1.0 fusion.27
  54.2 1.1 fusion.10
  55.3 0.7 broadcast_add_fusion
  56.0 1.2 convolution_convert_fusion.3
  57.2 39.1 %dispatch_rows.1 = bf16[32,40,768]{2,1,0:T(8,128)(2,1)S(1)} custom-call(bf16[8,40,768]{2,1,0:T(8,128)(2,1)S(1)} %bitcast.50), custom_call_target="tpu_custom_call" | custom-call | bytes 2457600 | tf_op jit(solution)/shard_map/dispatch_rows/pallas_call | solution.py:496
  96.3 0.4 copy.63
  96.7 0.1 fusion.52
  96.9 1.0 copy.64
  97.9 0.9 fusion.21
  98.9 1.0 copy.67
  99.9 0.3 copy-done.37
  100.2 1.9 fusion.9
  102.1 1.0 convolution_convert_fusion.1
  103.1 1.0 copy.69
  104.1 1.2 convolution_convert_fusion.2
  105.3 1.0 copy.66
  106.4 2.8 %maximum_bitcast_fusion = bf16[32,2,2,10,768]{4,2,3,0,1:T(2,128)(2,1)S(1)} fusion(bf16[1,2,32,10,768]{4,1,3,2,0:T(2,128)(2,1)S(1)} %bitcast.66, bf16[1,2,32,10,768]{4,1,3,2,0:T(2,128)(2,1)S(1)} %bitcast.67), kind=kLoop, calls=%fused_computation.13 | loop fusion | flops 983040 | bytes 3932160 | tf_op jit(solution)/shard_map/transpose | solution.py:730
  109.2 0.3 copy.70
  109.5 1.1 copy.71.part_ref
  110.7 34.8 %return_rows.1 = bf16[8,40,768]{2,1,0:T(8,128)(2,1)S(1)} custom-call(bf16[32,40,768]{2,1,0:T(8,128)(2,1)S(1)} %copy.71.part_ref), custom_call_target="tpu_custom_call" | custom-call | bytes 2457600 | tf_op jit(solution)/shard_map/return_rows/pallas_call | solution.py:496
  145.5 0.4 fusion.35
  145.9 0.8 fusion.28
  146.7 0.2 multiply_convert_fusion.2
  146.9 0.9 multiply_reduce_fusion
  147.8 0.2 fusion.51.branch_ref
  148.0 0.5 convolution_convert_fusion.4.grad_ref
  148.6 0.7 copy-done.3
  149.2 3.4 %attend_back.1 = (bf16[128,2304]{1,0:T(8,128)(2,1)S(1)}, f32[12,256]{1,0:T(8,128)S(1)}) custom-call(bf16[128,2304]{1,0:T(8,128)(2,1)S(1)} %convolution_convert_fusion.qkv_ref, f32[12,128,128]{2,1,0:T(8,128)S(1)} %copy-done.2, bf16[128,768]{1,0:T(8,128)(2,1)S(1)} %convolution_convert_fusion.4.grad_ref, bf16[128,128]{1,0:T(8,128)(2,1)S(1)} %copy-done.5), custom_call_target="tpu_custom_call" | custom-call | tf_op jit(solution)/shard_map/attend_back/pallas_call | solution.py:600
  152.7 1.4 fusion.26
  154.2 1.0 fusion.43
  155.2 0.2 copy.74.normed_ref
  155.4 0.2 copy.72
  155.6 1.1 fusion.72
  156.7 0.2 copy.75.ffn_ref
  156.9 1.2 fusion.54
  158.1 0.1 reshape.163
  158.3 0.9 copy-done.4
  159.2 1.1 copy-done.7
  160.3 35.3 %reduce_rows.1 = (f32[24,3200]{1,0:T(8,128)S(1)}, f32[16,128]{1,0:T(8,128)S(1)}) custom-call(bf16[768,128]{1,0:T(8,128)(2,1)S(1)} %copy.74.normed_ref, bf16[768,128]{1,0:T(8,128)(2,1)S(1)} %bitcast.51, bf16[768,128]{1,0:T(8,128)(2,1)S(1)} %copy.75.ffn_ref, bf16[128,2304]{1,0:T(8,128)(2,1)S(1)} %copy-done.7, bf16[128,768]{1,0:T(8,128)(2,1)S(1)} %copy-done.4, ...), custom_call_target="tpu_custom_call" | custom-call | flops 629145600 | bytes 307200 | tf_op jit(solution)/shard_map/reduce_rows/pallas_call | solution.py:306
  195.5 0.6 slice_bitcast_fusion
  196.1 0.7 slice.57
  196.8 0.6 slice.58
  197.6 0.7 copy.78
  198.3 0.7 copy.79
  198.9 5.3 %fusion.19 = f32[2,768,768]{2,1,0:T(8,128)} fusion(bf16[2,320,768]{2,1,0:T(8,128)(2,1)} %copy-done.16, bf16[2,320,768]{2,0,1:T(2,128)(2,1)} %bitcast.55), kind=kOutput, calls=%fused_computation.30 | convolution fusion | flops 754974720 | bytes 6684672 | tf_op jit(solution)/shard_map/lsd,lsf->ldf/dot_general | solution.py:724
  204.2 3.8 %fusion.13 = f32[2,768,768]{2,1,0:T(8,128)} fusion(bf16[2,320,768]{2,0,1:T(2,128)(2,1)S(1)} %bitcast.69, f32[2,320,768]{2,1,0:T(8,128)S(1)} %copy-done.11), kind=kOutput, calls=%fused_computation.26 | convolution fusion | flops 759398400 | bytes 7667712 | tf_op jit(solution)/shard_map/lsf,lsd->lfd/dot_general | solution.py:721
  (93 shorter events, 0.6 us)
Async XLA Ops:
  0.6 97.3 %copy-start = (bf16[2,768,768]{2,1,0:T(8,128)(2,1)S(1)}, bf16[2,768,768]{2,1,0:T(8,128)(2,1)}, u32[]{:S(2)}) copy-start(bf16[2,768,768]{2,1,0:T(8,128)(2,1)} %param.25) | copy-start | bytes 7077892
  3.2 33.2 %copy-start.17 = (bf16[128,768]{1,0:T(8,128)(2,1)S(1)}, bf16[128,768]{1,0:T(8,128)(2,1)}, u32[]{:S(2)}) copy-start(bf16[128,768]{1,0:T(8,128)(2,1)} %param.15) | copy-start | bytes 589828
  3.2 33.8 %copy-start.31 = (f32[768]{0:T(1024)S(1)}, f32[768]{0:T(1024)}, u32[]{:S(2)}) copy-start(f32[768]{0:T(1024)} %param.19) | copy-start | bytes 9220
  36.5 0.5 copy-start.35
  37.1 2.8 %copy-start.33 = (f32[128]{0:T(128)}, f32[128]{0:T(128)S(1)}, u32[]{:S(2)}) copy-start(f32[128]{0:T(128)S(1)} %fusion.48) | copy-start | bytes 1540
  37.1 2.8 %copy-start.38 = (s32[1,3]{1,0:T(1,128)S(1)}, s32[1,3]{1,0:T(1,128)}, u32[]{:S(2)}) copy-start(s32[1,3]{1,0:T(1,128)} %param.17) | copy-start | bytes 40
  37.1 3.2 %copy-start.20 = (f32[256,32]{1,0:T(8,128)S(1)}, f32[256,32]{1,0:T(8,128)}, u32[]{:S(2)}) copy-start(f32[256,32]{1,0:T(8,128)} %constant.59.clone) | copy-start | bytes 98308
  37.1 3.2 %copy-start.29 = (f32[32,12]{0,1:T(8,128)S(1)}, f32[32,12]{0,1:T(8,128)}, u32[]{:S(2)}) copy-start(f32[32,12]{0,1:T(8,128)} %param.22) | copy-start | bytes 4612
  39.8 8.1 %copy-start.23 = (f32[768]{0:T(1024)S(1)}, f32[768]{0:T(1024)}, u32[]{:S(2)}) copy-start(f32[768]{0:T(1024)} %param.23) | copy-start | bytes 9220
  44.8 0.9 copy-start.1
  47.4 0.5 copy-start.39
  47.4 106.8 %copy-start.8 = (f32[128,768]{1,0:T(8,128)}, f32[128,768]{1,0:T(8,128)S(1)}, u32[]{:S(2)}) copy-start(f32[128,768]{1,0:T(8,128)S(1)} %get-tuple-element.67) | copy-start | bytes 1179652
  47.9 99.9 %copy-start.26 = (f32[128]{0:T(128)}, f32[128]{0:T(128)S(1)}, u32[]{:S(2)}) copy-start(f32[128]{0:T(128)S(1)} %fusion.49) | copy-start | bytes 1540
  48.0 0.7 copy-start.19
  97.9 1.0 copy-start.9
  97.9 2.3 %copy-start.37 = (bf16[2,768,768]{2,1,0:T(8,128)(2,1)S(1)}, bf16[2,768,768]{2,1,0:T(8,128)(2,1)}, u32[]{:S(2)}) copy-start(bf16[2,768,768]{2,1,0:T(8,128)(2,1)} %param.26) | copy-start | bytes 7077892
  98.9 5.2 %copy-start.10 = (f32[2,320,768]{2,1,0:T(8,128)}, f32[2,320,768]{2,1,0:T(8,128)S(1)}, u32[]{:S(2)}) copy-start(f32[2,320,768]{2,1,0:T(8,128)S(1)} %fusion.21) | copy-start | bytes 5898244
  99.9 2.2 %copy-start.12 = (bf16[1,2,32,10,768]{4,1,3,2,0:T(2,128)(2,1)}, bf16[1,2,32,10,768]{4,1,3,2,0:T(2,128)(2,1)S(1)}, u32[]{:S(2)}) copy-start(bf16[1,2,32,10,768]{4,1,3,2,0:T(2,128)(2,1)S(1)} %copy.67) | copy-start | bytes 2949124
  102.1 1.0 copy-start.16
  109.2 37.7 %slice-start = ((s8[4915200]{0:T(1024)(128)(4,1)}), s8[4194304]{0:T(1024)(128)(4,1)S(1)}, s32[]{:S(2)}) async-start(s8[4915200]{0:T(1024)(128)(4,1)} %bitcast.61), calls=%async_computation | async-start | bytes 8388608
  109.5 37.4 %slice-start.1 = ((s8[4915200]{0:T(1024)(128)(4,1)}), s8[720896]{0:T(1024)(128)(4,1)S(1)}, s32[]{:S(2)}) async-start(s8[4915200]{0:T(1024)(128)(4,1)} %bitcast.61), calls=%async_computation.1 | async-start | bytes 1441792
  110.6 35.3 %copy-start.14 = (bf16[128,768]{1,0:T(8,128)(2,1)S(1)}, bf16[128,768]{1,0:T(8,128)(2,1)}, u32[]{:S(2)}) copy-start(bf16[128,768]{1,0:T(8,128)(2,1)} %param.16) | copy-start | bytes 589828
  110.6 36.1 %copy-start.15 = (f32[128,16]{1,0:T(8,128)S(1)}, f32[128,16]{1,0:T(8,128)}, u32[]{:S(2)}) copy-start(f32[128,16]{1,0:T(8,128)} %copy.61) | copy-start | bytes 24580
  110.6 36.1 %copy-start.28 = (f32[128]{0:T(128)S(1)}, f32[128]{0:T(128)}, u32[]{:S(2)}) copy-start(f32[128]{0:T(128)} %get-tuple-element.68) | copy-start | bytes 1540
  110.6 36.1 %copy-start.30 = (s32[128,1]{0,1:T(1,128)S(1)}, s32[128,1]{0,1:T(1,128)}, u32[]{:S(2)}) copy-start(s32[128,1]{0,1:T(1,128)} %param.18) | copy-start | bytes 1540
  145.5 2.3 %copy-start.40 = (f32[128]{0:T(128)S(1)}, f32[128]{0:T(128)}, u32[]{:S(2)}) copy-start(f32[128]{0:T(128)} %copy-done.39) | copy-start | bytes 1540
  146.9 0.9 copy-start.21
  146.9 2.3 %copy-start.2 = (f32[12,128,128]{2,1,0:T(8,128)S(1)}, f32[12,128,128]{2,1,0:T(8,128)}, u32[]{:S(2)}) copy-start(f32[12,128,128]{2,1,0:T(8,128)} %copy-done.1) | copy-start | bytes 2359300
  146.9 2.3 %copy-start.5 = (bf16[128,128]{1,0:T(8,128)(2,1)S(1)}, bf16[128,128]{1,0:T(8,128)(2,1)}, u32[]{:S(2)}) copy-start(bf16[128,128]{1,0:T(8,128)(2,1)} %constant.61.clone.flip_ref) | copy-start | bytes 98308
  148.0 4.7 %copy-start.18 = (bf16[128,768]{1,0:T(8,128)(2,1)S(1)}, bf16[128,768]{1,0:T(8,128)(2,1)}, u32[]{:S(2)}) copy-start(bf16[128,768]{1,0:T(8,128)(2,1)} %param.15) | copy-start | bytes 589828
  148.0 4.7 %copy-start.32 = (f32[768]{0:T(1024)S(1)}, f32[768]{0:T(1024)}, u32[]{:S(2)}) copy-start(f32[768]{0:T(1024)} %param.19) | copy-start | bytes 9220
  148.0 4.7 %copy-start.34 = (f32[128]{0:T(128)S(1)}, f32[128]{0:T(128)}, u32[]{:S(2)}) copy-start(f32[128]{0:T(128)} %copy-done.33) | copy-start | bytes 1540
  148.6 0.7 copy-start.3
  152.7 1.5 copy-start.6
  152.7 1.4 copy-start.36
  152.7 1.5 copy-start.24
  152.7 1.5 copy-start.27
  154.2 2.7 %copy-start.22 = (bf16[128,16]{1,0:T(8,128)(2,1)S(1)}, bf16[128,16]{1,0:T(8,128)(2,1)}, u32[]{:S(2)}) copy-start(bf16[128,16]{1,0:T(8,128)(2,1)} %copy-done.21) | copy-start | bytes 12292
  154.2 4.0 %copy-start.25 = (f32[768]{0:T(1024)S(1)}, f32[768]{0:T(1024)}, u32[]{:S(2)}) copy-start(f32[768]{0:T(1024)} %get-tuple-element.52) | copy-start | bytes 9220
  158.3 0.9 copy-start.4
  159.2 1.1 copy-start.7
  198.9 5.3 %copy-start.11 = (f32[2,320,768]{2,1,0:T(8,128)S(1)}, f32[2,320,768]{2,1,0:T(8,128)}, u32[]{:S(2)}) copy-start(f32[2,320,768]{2,1,0:T(8,128)} %copy-done.10) | copy-start | bytes 5898244
  198.9 5.3 %copy-start.13 = (bf16[1,2,32,10,768]{4,1,3,2,0:T(2,128)(2,1)S(1)}, bf16[1,2,32,10,768]{4,1,3,2,0:T(2,128)(2,1)}, u32[]{:S(2)}) copy-start(bf16[1,2,32,10,768]{4,1,3,2,0:T(2,128)(2,1)} %copy-done.12) | copy-start | bytes 2949124

commit v4 on v3

--- a/solution.py
+++ b/solution.py
@@ -160,7 +160,7 @@
 
 def reduce_kernel(
     normed_ref, attended_ref, ffn_ref, qkv_ref, branch_ref, logit_ref, small_ref,
-    out_ref, total_ref,
+    out_qkv_ref, out_out_ref, out_route_ref, total_ref,
     grad_ref, from_core, summed, passing, from_x, from_y, from_z,
     small_sum, small_in, small_z, send_sem, recv_sem, small_send, small_recv,
 ):
@@ -255,7 +255,10 @@
         if j == 0:
             for other in (1, 2, 3):
                 value = value + arrive(from_z.at[other - 1], 27 + other)
-            out_ref[...] = value
+            column = 0
+            for owned_ref in (out_qkv_ref, out_out_ref, out_route_ref):
+                owned_ref[...] = value[:, column : column + owned_ref.shape[1]]
+                column += owned_ref.shape[1]
         else:
             summed[j] = value.astype(jnp.bfloat16)
             send(summed.at[j], from_z.at[3 - j], along[j], 31 - j)
@@ -305,12 +308,12 @@
     block = functools.partial(pltpu.VMEM, dtype=jnp.bfloat16)
     return pl.pallas_call(
         reduce_kernel,
-        out_shape=(
-            jax.ShapeDtypeStruct((rows, width), jnp.float32),
-            jax.ShapeDtypeStruct(small.shape, jnp.float32),
-        ),
+        out_shape=tuple(
+            jax.ShapeDtypeStruct((rows, right.shape[1]), jnp.float32) for right in operands[3:]
+        )
+        + (jax.ShapeDtypeStruct(small.shape, jnp.float32),),
         in_specs=[vmem] * 7,
-        out_specs=(vmem, vmem),
+        out_specs=(vmem,) * 4,
         scratch_shapes=[
             block((32, rows, width)),
             block((16, rows, width)),
@@ -778,7 +781,7 @@
         small_size = small.shape[0]
         small_rows = -(-small_size // (8 * lane_count)) * 8
         small = jnp.pad(small, (0, small_rows * lane_count - small_size))
-        owned, small = reduce_rows(
+        grad_attn_qkv, grad_attn_out, grad_router, small = reduce_rows(
             [left.T for left, _ in dense_pairs] + [right for _, right in dense_pairs],
             shard_rows,
             small.reshape(small_rows, lane_count),
@@ -812,9 +815,10 @@
         grad_gain_attn, grad_gain_ffn, grad_bias = lax.psum(
             (grad_gain_attn, grad_gain_ffn, grad_bias), ("exp", "dp")
         )
-    grad_attn_qkv = owned[:, : 3 * model_width]
-    grad_attn_out = owned[:, 3 * model_width : 4 * model_width]
-    grad_router = owned[:, 4 * model_width : dense_width]
+        grad_attn_qkv = owned[:, : 3 * model_width]
+        grad_attn_out = owned[:, 3 * model_width : 4 * model_width]
+        grad_router = owned[:, 4 * model_width :]
+    grad_router = grad_router[:, :expert_count]
     return (
         mixed,
         grad_in,

time: 209 us -> 209 us (level)
    unnamed x89 -> x83, local copies, waits for them, and re-layouts: 7.93 us -> 7.63 us
where the time goes in v4:
time: 209 us
  Pallas kernels  150 us (72%)
  matrix products  27.6 us (13%)
  local copies, waits for them, and re-layouts  18.2 us (9%)
  other arithmetic  11.3 us (5%)
    pallas_call x2, Pallas kernels, line_call(): pl.pallas_call(kernel, out_shape=jax.ShapeDtypeStruct((blocks, rows, widt...  73.9 us
    pallas_call x1, Pallas kernels, reduce_rows(): pl.pallas_call(reduce_kernel, out_shape=tuple((jax.ShapeDtypeStruct((rows...  35.3 us
    pallas_call x1, Pallas kernels, gather_rows(): pl.pallas_call(gather_kernel, out_shape=jax.ShapeDtypeStruct((32, rows, w...  33.2 us
    pallas_call x2, Pallas kernels, attention_call(): pl.pallas_call(kernel, out_shape=shapes, in_specs=[vmem] * len(operands),...  7.74 us
    unnamed x83, local copies, waits for them, and re-layouts  7.63 us
    dot_general x1, matrix products, local(): jnp.einsum('lsd,lsf->ldf', expert_rows, grad_pre, preferred_element_type=...  5.27 us

profile of v4, /device:TPU:0, one launch (start us, length us, event | category | flops | bytes accessed | tf_op | source)
XLA Modules:
  0.0 208.6 jit_solution(7163382924033710127)
XLA Ops:
  0.7 0.9 copy.59
  1.6 1.6 concatenate.13.mine_ref
  3.2 33.2 %gather_rows.1 = bf16[32,24,3200]{2,1,0:T(8,128)(2,1)} custom-call(bf16[24,3200]{1,0:T(8,128)(2,1)} %concatenate.13.mine_ref), custom_call_target="tpu_custom_call" | custom-call | bytes 4915200 | tf_op jit(solution)/shard_map/gather_rows/pallas_call | solution.py:144
  36.4 0.1 fusion.30
  36.5 0.5 copy-done.31
  37.1 2.7 %convolution_convert_fusion.qkv_ref = bf16[128,2304]{1,0:T(8,128)(2,1)S(1)} fusion(bf16[768,3200]{1,0:T(8,128)(2,1)} %bitcast.60, bf16[128,768]{1,0:T(8,128)(2,1)S(1)} %copy-done.16, f32[768]{0:T(1024)S(1)} %copy-done.26, f32[128]{0:T(128)S(1)} %fusion.48), kind=kOutput, calls=%fused_computation | convolution fusion | flops 453672960 | bytes 4328960 | tf_op jit(solution)/shard_map/dot_general | solution.py:658
  39.8 0.2 reduce_window_sum.11
  40.1 0.1 copy.60.column_ref
  40.2 0.2 convolution_bitcast_fusion.offset_ref
  40.5 4.3 %attend.1 = (bf16[128,768]{1,0:T(8,128)(2,1)S(1)}, f32[12,128,128]{2,1,0:T(8,128)S(1)}) custom-call(bf16[128,2304]{1,0:T(8,128)(2,1)S(1)} %convolution_convert_fusion.qkv_ref, s32[128,1]{1,0:T(8,128)S(1)} %copy.60.column_ref, s32[1,128]{1,0:T(1,128)S(1)} %bitcast.55, f32[12,256]{1,0:T(8,128)S(1)} %convolution_bitcast_fusion.offset_ref), custom_call_target="tpu_custom_call" | custom-call | tf_op jit(solution)/shard_map/attend/pallas_call | solution.py:603
  44.8 0.9 copy-done.1
  45.7 1.7 multiply_reduce_fusion.2
  47.4 0.5 copy-done.35
  48.0 0.7 copy-done.18
  48.7 1.7 fusion.53
  50.4 0.7 copy.61
  51.1 1.0 fusion.42
  52.1 1.0 select_reduce_fusion
  53.2 1.0 fusion.27
  54.2 1.1 fusion.10
  55.3 0.7 broadcast_add_fusion
  56.0 1.2 convolution_convert_fusion.3
  57.2 39.1 %dispatch_rows.1 = bf16[32,40,768]{2,1,0:T(8,128)(2,1)S(1)} custom-call(bf16[8,40,768]{2,1,0:T(8,128)(2,1)S(1)} %bitcast.51), custom_call_target="tpu_custom_call" | custom-call | bytes 2457600 | tf_op jit(solution)/shard_map/dispatch_rows/pallas_call | solution.py:499
  96.3 0.4 copy.63
  96.8 0.1 fusion.52
  96.9 1.0 copy.64
  98.0 0.9 fusion.21
  98.9 1.0 copy.67
  99.9 0.3 copy-done.33
  100.2 1.9 fusion.9
  102.1 1.0 convolution_convert_fusion.1
  103.1 1.0 copy.69
  104.1 1.2 convolution_convert_fusion.2
  105.4 1.0 copy.66
  106.4 2.8 %maximum_bitcast_fusion = bf16[32,2,2,10,768]{4,2,3,0,1:T(2,128)(2,1)S(1)} fusion(bf16[1,2,32,10,768]{4,1,3,2,0:T(2,128)(2,1)S(1)} %bitcast.68, bf16[1,2,32,10,768]{4,1,3,2,0:T(2,128)(2,1)S(1)} %bitcast.69), kind=kLoop, calls=%fused_computation.13 | loop fusion | flops 983040 | bytes 3932160 | tf_op jit(solution)/shard_map/transpose | solution.py:733
  109.2 0.3 copy.70
  109.5 1.1 copy.71.part_ref
  110.7 34.8 %return_rows.1 = bf16[8,40,768]{2,1,0:T(8,128)(2,1)S(1)} custom-call(bf16[32,40,768]{2,1,0:T(8,128)(2,1)S(1)} %copy.71.part_ref), custom_call_target="tpu_custom_call" | custom-call | bytes 2457600 | tf_op jit(solution)/shard_map/return_rows/pallas_call | solution.py:499
  145.5 0.4 fusion.35
  145.9 0.8 fusion.28
  146.7 0.2 multiply_convert_fusion.2
  146.9 0.9 multiply_reduce_fusion
  147.8 1.2 fusion.51.branch_ref
  149.0 0.5 convolution_convert_fusion.4.grad_ref
  149.6 3.4 %attend_back.1 = (bf16[128,2304]{1,0:T(8,128)(2,1)S(1)}, f32[12,256]{1,0:T(8,128)S(1)}) custom-call(bf16[128,2304]{1,0:T(8,128)(2,1)S(1)} %convolution_convert_fusion.qkv_ref, f32[12,128,128]{2,1,0:T(8,128)S(1)} %copy-done.2, bf16[128,768]{1,0:T(8,128)(2,1)S(1)} %convolution_convert_fusion.4.grad_ref, bf16[128,128]{1,0:T(8,128)(2,1)S(1)} %copy-done.3), custom_call_target="tpu_custom_call" | custom-call | tf_op jit(solution)/shard_map/attend_back/pallas_call | solution.py:603
  153.0 1.9 fusion.26
  155.0 1.0 fusion.43
  156.0 0.2 copy.74.normed_ref
  156.2 0.2 copy.72
  156.3 1.1 fusion.72
  157.4 0.2 copy.75.ffn_ref
  157.6 0.8 pad.8.logit_ref
  158.4 1.2 fusion.54
  159.6 0.1 reshape.163
  159.8 1.1 copy-done.5
  160.9 35.3 %reduce_rows.1 = (f32[24,2304]{1,0:T(8,128)S(1)}, f32[24,768]{1,0:T(8,128)S(1)}, f32[24,128]{1,0:T(8,128)S(1)}, f32[16,128]{1,0:T(8,128)S(1)}) custom-call(bf16[768,128]{1,0:T(8,128)(2,1)S(1)} %copy.74.normed_ref, bf16[768,128]{1,0:T(8,128)(2,1)S(1)} %bitcast.52, bf16[768,128]{1,0:T(8,128)(2,1)S(1)} %copy.75.ffn_ref, bf16[128,2304]{1,0:T(8,128)(2,1)S(1)} %copy-done.5, ...), custom_call_target="tpu_custom_call" | custom-call | flops 629145600 | bytes 307200 | tf_op jit(solution)/shard_map/reduce_rows/pallas_call | solution.py:309
  196.2 0.6 slice_bitcast_fusion
  196.8 0.1 reshape.165
  196.9 0.7 copy.78
  197.6 0.7 copy.79
  198.2 5.3 %fusion.19 = f32[2,768,768]{2,1,0:T(8,128)} fusion(bf16[2,320,768]{2,1,0:T(8,128)(2,1)} %copy-done.15, bf16[2,320,768]{2,0,1:T(2,128)(2,1)} %bitcast.57), kind=kOutput, calls=%fused_computation.30 | convolution fusion | flops 754974720 | bytes 6684672 | tf_op jit(solution)/shard_map/lsd,lsf->ldf/dot_general | solution.py:727
  203.5 3.8 %fusion.13 = f32[2,768,768]{2,1,0:T(8,128)} fusion(bf16[2,320,768]{2,0,1:T(2,128)(2,1)S(1)} %bitcast.71, f32[2,320,768]{2,1,0:T(8,128)S(1)} %copy-done.10), kind=kOutput, calls=%fused_computation.26 | convolution fusion | flops 759398400 | bytes 7667712 | tf_op jit(solution)/shard_map/lsf,lsd->lfd/dot_general | solution.py:724
  207.3 0.7 copy.94
  208.0 0.6 copy.95
  (84 shorter events, 0.5 us)
Async XLA Ops:
  0.6 97.3 %copy-start = (bf16[2,768,768]{2,1,0:T(8,128)(2,1)S(1)}, bf16[2,768,768]{2,1,0:T(8,128)(2,1)}, u32[]{:S(2)}) copy-start(bf16[2,768,768]{2,1,0:T(8,128)(2,1)} %param.25) | copy-start | bytes 7077892
  3.2 33.2 %copy-start.16 = (bf16[128,768]{1,0:T(8,128)(2,1)S(1)}, bf16[128,768]{1,0:T(8,128)(2,1)}, u32[]{:S(2)}) copy-start(bf16[128,768]{1,0:T(8,128)(2,1)} %param.15) | copy-start | bytes 589828
  3.2 33.8 %copy-start.26 = (f32[768]{0:T(1024)S(1)}, f32[768]{0:T(1024)}, u32[]{:S(2)}) copy-start(f32[768]{0:T(1024)} %param.19) | copy-start | bytes 9220
  36.5 0.5 copy-start.31
  37.1 2.8 %copy-start.29 = (f32[128]{0:T(128)}, f32[128]{0:T(128)S(1)}, u32[]{:S(2)}) copy-start(f32[128]{0:T(128)S(1)} %fusion.48) | copy-start | bytes 1540
  37.1 2.8 %copy-start.34 = (s32[1,3]{1,0:T(1,128)S(1)}, s32[1,3]{1,0:T(1,128)}, u32[]{:S(2)}) copy-start(s32[1,3]{1,0:T(1,128)} %param.17) | copy-start | bytes 40
  37.1 3.2 %copy-start.19 = (f32[256,32]{1,0:T(8,128)S(1)}, f32[256,32]{1,0:T(8,128)}, u32[]{:S(2)}) copy-start(f32[256,32]{1,0:T(8,128)} %constant.59.clone) | copy-start | bytes 98308
  37.1 3.2 %copy-start.24 = (f32[32,12]{0,1:T(8,128)S(1)}, f32[32,12]{0,1:T(8,128)}, u32[]{:S(2)}) copy-start(f32[32,12]{0,1:T(8,128)} %param.22) | copy-start | bytes 4612
  39.8 8.1 %copy-start.21 = (f32[768]{0:T(1024)S(1)}, f32[768]{0:T(1024)}, u32[]{:S(2)}) copy-start(f32[768]{0:T(1024)} %param.23) | copy-start | bytes 9220
  44.8 0.9 copy-start.1
  47.4 0.5 copy-start.35
  47.4 99.5 %copy-start.6 = (f32[128,768]{1,0:T(8,128)}, f32[128,768]{1,0:T(8,128)S(1)}, u32[]{:S(2)}) copy-start(f32[128,768]{1,0:T(8,128)S(1)} %get-tuple-element.71) | copy-start | bytes 1179652
  48.0 0.7 copy-start.18
  97.9 1.0 copy-start.8
  97.9 2.3 %copy-start.33 = (bf16[2,768,768]{2,1,0:T(8,128)(2,1)S(1)}, bf16[2,768,768]{2,1,0:T(8,128)(2,1)}, u32[]{:S(2)}) copy-start(bf16[2,768,768]{2,1,0:T(8,128)(2,1)} %param.26) | copy-start | bytes 7077892
  98.9 5.2 %copy-start.9 = (f32[2,320,768]{2,1,0:T(8,128)}, f32[2,320,768]{2,1,0:T(8,128)S(1)}, u32[]{:S(2)}) copy-start(f32[2,320,768]{2,1,0:T(8,128)S(1)} %fusion.21) | copy-start | bytes 5898244
  99.9 2.2 %copy-start.11 = (bf16[1,2,32,10,768]{4,1,3,2,0:T(2,128)(2,1)}, bf16[1,2,32,10,768]{4,1,3,2,0:T(2,128)(2,1)S(1)}, u32[]{:S(2)}) copy-start(bf16[1,2,32,10,768]{4,1,3,2,0:T(2,128)(2,1)S(1)} %copy.67) | copy-start | bytes 2949124
  102.1 1.0 copy-start.15
  109.2 37.7 %slice-start = ((s8[4915200]{0:T(1024)(128)(4,1)}), s8[4194304]{0:T(1024)(128)(4,1)S(1)}, s32[]{:S(2)}) async-start(s8[4915200]{0:T(1024)(128)(4,1)} %bitcast.63), calls=%async_computation | async-start | bytes 8388608
  109.5 37.4 %slice-start.1 = ((s8[4915200]{0:T(1024)(128)(4,1)}), s8[720896]{0:T(1024)(128)(4,1)S(1)}, s32[]{:S(2)}) async-start(s8[4915200]{0:T(1024)(128)(4,1)} %bitcast.63), calls=%async_computation.1 | async-start | bytes 1441792
  110.6 35.3 %copy-start.13 = (bf16[128,768]{1,0:T(8,128)(2,1)S(1)}, bf16[128,768]{1,0:T(8,128)(2,1)}, u32[]{:S(2)}) copy-start(bf16[128,768]{1,0:T(8,128)(2,1)} %param.16) | copy-start | bytes 589828
  110.6 36.1 %copy-start.14 = (f32[128,16]{1,0:T(8,128)S(1)}, f32[128,16]{1,0:T(8,128)}, u32[]{:S(2)}) copy-start(f32[128,16]{1,0:T(8,128)} %copy.61) | copy-start | bytes 24580
  110.7 36.0 %copy-start.23 = (f32[128]{0:T(128)S(1)}, f32[128]{0:T(128)}, u32[]{:S(2)}) copy-start(f32[128]{0:T(128)} %get-tuple-element.72) | copy-start | bytes 1540
  110.7 36.0 %copy-start.25 = (s32[128,1]{0,1:T(1,128)S(1)}, s32[128,1]{0,1:T(1,128)}, u32[]{:S(2)}) copy-start(s32[128,1]{0,1:T(1,128)} %param.18) | copy-start | bytes 1540
  145.5 2.3 %copy-start.36 = (f32[128]{0:T(128)S(1)}, f32[128]{0:T(128)}, u32[]{:S(2)}) copy-start(f32[128]{0:T(128)} %copy-done.35) | copy-start | bytes 1540
  146.9 0.9 copy-start.20
  146.9 2.6 %copy-start.2 = (f32[12,128,128]{2,1,0:T(8,128)S(1)}, f32[12,128,128]{2,1,0:T(8,128)}, u32[]{:S(2)}) copy-start(f32[12,128,128]{2,1,0:T(8,128)} %copy-done.1) | copy-start | bytes 2359300
  146.9 2.6 %copy-start.3 = (bf16[128,128]{1,0:T(8,128)(2,1)S(1)}, bf16[128,128]{1,0:T(8,128)(2,1)}, u32[]{:S(2)}) copy-start(bf16[128,128]{1,0:T(8,128)(2,1)} %constant.61.clone.flip_ref) | copy-start | bytes 98308
  149.0 4.0 %copy-start.17 = (bf16[128,768]{1,0:T(8,128)(2,1)S(1)}, bf16[128,768]{1,0:T(8,128)(2,1)}, u32[]{:S(2)}) copy-start(bf16[128,768]{1,0:T(8,128)(2,1)} %param.15) | copy-start | bytes 589828
  149.0 4.0 %copy-start.27 = (f32[768]{0:T(1024)S(1)}, f32[768]{0:T(1024)}, u32[]{:S(2)}) copy-start(f32[768]{0:T(1024)} %param.19) | copy-start | bytes 9220
  149.0 4.0 %copy-start.30 = (f32[128]{0:T(128)S(1)}, f32[128]{0:T(128)}, u32[]{:S(2)}) copy-start(f32[128]{0:T(128)} %copy-done.29) | copy-start | bytes 1540
  153.0 2.0 copy-start.4
  153.0 1.9 copy-start.32
  153.0 1.9 copy-start.7
  156.0 3.8 %copy-start.22 = (f32[768]{0:T(1024)S(1)}, f32[768]{0:T(1024)}, u32[]{:S(2)}) copy-start(f32[768]{0:T(1024)} %get-tuple-element.56) | copy-start | bytes 9220
  156.0 3.8 %copy-start.28 = (f32[768]{0:T(1024)S(1)}, f32[768]{0:T(1024)}, u32[]{:S(2)}) copy-start(f32[768]{0:T(1024)} %get-tuple-element.58) | copy-start | bytes 9220
  159.8 1.1 copy-start.5
  198.2 5.3 %copy-start.10 = (f32[2,320,768]{2,1,0:T(8,128)S(1)}, f32[2,320,768]{2,1,0:T(8,128)}, u32[]{:S(2)}) copy-start(f32[2,320,768]{2,1,0:T(8,128)} %copy-done.9) | copy-start | bytes 5898244
  198.2 5.3 %copy-start.12 = (bf16[1,2,32,10,768]{4,1,3,2,0:T(2,128)(2,1)S(1)}, bf16[1,2,32,10,768]{4,1,3,2,0:T(2,128)(2,1)}, u32[]{:S(2)}) copy-start(bf16[1,2,32,10,768]{4,1,3,2,0:T(2,128)(2,1)} %copy-done.11) | copy-start | bytes 2949124
